TPU v7x, 256 devices: a whole 4x4x8 slice. The times are simulated.
256 devices in a mesh: dp: 32 (over z, y), mp: 8 (over x, core).
Axes of the slice: x: 4, y: 4, z: 8, core: 2. Of those that a mesh axis runs over, the one named last changes fastest.
Arguments:
- gradients: bfloat16 [32, 1536, 5120], P('dp', 'mp')
- errors: float32 [32, 1536, 5120], P('dp', 'mp'), may hold values from -3 to 3
- seed_table: int32 [5120, 32], replicated, may hold values from -1006 to 1006
Outputs:
- new_errors: float32 [32, 1536, 5120], P('dp', 'mp')
- update: bfloat16 [1536, 5120], P('mp')
- right_factor: float32 [5120, 32], replicated
- left_factor: float32 [1536, 32], P('mp')
All inputs are finite; a program needn't handle non-finite values.
Results may differ from a plain program's by a relative error of at most 0.0015.
Values sent between devices are 32-bit elements; how exact they have to be, the bound alone decides.
A program may use at most 64 MiB of HBM per device.

v0:
```python
import jax
import jax.numpy as jnp
from jax import lax
from jax.sharding import PartitionSpec as P


def cholesky_step(left, gram_matrix):
    lower = jnp.linalg.cholesky(gram_matrix)
    return jax.scipy.linalg.solve_triangular(lower, left.T, lower=True).T


def local_gram(left):
    return jnp.dot(
        left.T, left, precision=lax.Precision.HIGHEST, preferred_element_type=jnp.float32
    )


def local(gradients, errors, seed_table):
    merged = gradients[0].astype(jnp.float32) + errors[0]
    start = seed_table.astype(jnp.float32) / 1000.0
    left_local = jnp.dot(
        merged, start, precision=lax.Precision.HIGHEST, preferred_element_type=jnp.float32
    )
    left_sum = lax.psum(left_local, "dp")
    left_factor = left_sum
    for passes in range(2):
        gram_matrix = lax.psum(local_gram(left_factor), "mp")
        left_factor = cholesky_step(left_factor, gram_matrix)
    right_local = lax.dot_general(
        merged,
        left_factor,
        (((0,), (0,)), ((), ())),
        precision=lax.Precision.HIGHEST,
        preferred_element_type=jnp.float32,
    )
    replicas = lax.axis_size("dp")
    right_total = lax.psum(right_local, ("dp", "mp"))
    right_factor = right_total / replicas
    approx = jnp.dot(
        left_factor,
        right_factor.T,
        precision=lax.Precision.HIGHEST,
        preferred_element_type=jnp.float32,
    )
    new_errors = (merged - approx)[None]
    return (new_errors, approx.astype(jnp.bfloat16), right_factor, left_factor)


def solution(mesh):
    in_specs = (P("dp", "mp", None), P("dp", "mp", None), P())
    out_specs = (P("dp", "mp", None), P("mp", None), P(), P("mp", None))
    return jax.shard_map(local, mesh=mesh, in_specs=in_specs, out_specs=out_specs, check_vma=False)
```

profile of v0, /device:TPU:1, one launch (start us, length us, event | category | flops | bytes accessed | tf_op | source)
XLA Modules:
  0.0 486.6 jit_solution(12419941020870407972)
XLA Ops:
  7.2 0.0 copy-start
  7.2 0.0 all-reduce.2.cloned.1.call-start
  7.2 6.5 %fusion.2 = f32[192,32]{0,1:T(8,128)S(1)} fusion(f32[1,192,5120]{2,1,0:T(8,128)} %param.7, bf16[1,192,5120]{2,1,0:T(8,128)(2,1)} %param.6, s32[5120,32]{0,1:T(8,128)} %param.8), kind=kOutput, calls=%fused_computation.3 | convolution fusion | flops 379781120 | bytes 6578176 | tf_op jit(solution)/shard_map/dot_general | solution.py:21
  13.8 118.9 %psum.28 = f32[192,32]{0,1:T(8,128)S(1)} all-reduce(f32[192,32]{0,1:T(8,128)S(1)} %fusion.2), channel_id=1, replica_groups=mesh['dp'=32,'mp'=8] {'dp'}, use_global_device_ids=true, to_apply=%region_0.0 | all-reduce | flops 6144 | bytes 49152 | tf_op jit(solution)/shard_map/psum | solution.py:24
  132.7 0.2 fusion.21
  132.9 48.5 %psum.29 = f32[32,32]{0,1:T(8,128)S(1)} all-reduce(f32[32,32]{0,1:T(8,128)S(1)} %fusion.21), channel_id=1, replica_groups=mesh['dp'=32,'mp'=8] {'mp'}, use_global_device_ids=true, to_apply=%region_1.0 | all-reduce | flops 1024 | bytes 8192 | tf_op jit(solution)/shard_map/psum | solution.py:27
  181.4 0.1 copy.8
  181.5 2.9 cholesky.44
  184.4 0.6 compare_reduce_fusion.1
  185.1 0.7 fusion.10
  185.7 2.4 custom-call.6
  188.2 0.2 fusion.8
  188.4 0.2 fusion.22
  188.6 23.6 %psum.30 = f32[32,32]{0,1:T(8,128)S(1)} all-reduce(f32[32,32]{0,1:T(8,128)S(1)} %fusion.22), channel_id=1, replica_groups=mesh['dp'=32,'mp'=8] {'mp'}, use_global_device_ids=true, to_apply=%region_4.7 | all-reduce | flops 1024 | bytes 8192 | tf_op jit(solution)/shard_map/psum | solution.py:27
  212.2 0.1 copy.10
  212.2 2.9 cholesky.55
  215.2 0.6 compare_reduce_fusion
  215.8 0.7 fusion.11
  216.5 2.4 custom-call.7
  218.9 0.2 fusion.12
  219.2 0.0 copy-done
  219.2 0.0 copy-start.2
  219.2 5.4 %fusion = f32[5120,32]{0,1:T(8,128)} fusion(f32[32,192]{1,0:T(8,128)S(1)} %fusion.12, f32[1,192,5120]{2,1,0:T(8,128)} %param.7, bf16[1,192,5120]{2,1,0:T(8,128)(2,1)S(1)} %copy-done), kind=kOutput, calls=%fused_computation.1 | convolution fusion | flops 379453440 | bytes 6578176 | tf_op jit(solution)/shard_map/dot_general | solution.py:29
  224.6 0.0 all-reduce.2.cloned.1.call-update
  224.6 246.8 %all-reduce.2.cloned.1.call-done = f32[5120,32]{0,1:T(8,128)} async-done(((f32[5120,32]{0,1:T(8,128)}), f32[5120,32]{0,1:T(8,128)}) %all-reduce.2.cloned.1.call-update) | async-done | bytes 655376 | tf_op jit(solution)/shard_map/psum | solution.py:37
  471.4 1.1 broadcast_multiply_fusion
  472.5 0.0 copy-done.2
  472.5 0.0 copy-start.1
  472.5 7.2 %fusion.20 = (bf16[192,5120]{1,0:T(8,128)(2,1)}, f32[1,192,5120]{2,1,0:T(8,128)}) fusion(f32[1,192,5120]{2,1,0:T(8,128)} %param.7, bf16[1,192,5120]{2,1,0:T(8,128)(2,1)S(1)} %copy-done, f32[32,192]{1,0:T(8,128)S(1)} %fusion.12, f32[5120,32]{0,1:T(8,128)S(1)} %broadcast_multiply_fusion), kind=kOutput, calls=%fused_computation.32 | convolution fusion | flops 381419520 | bytes 12476416 | tf_op jit(solution)/shard_map/dot_general | solution.py:39
  479.8 0.0 copy-done.1
  (4 shorter events, 0.1 us)
Async XLA Ops:
  7.2 212.0 %copy-start = (bf16[1,192,5120]{2,1,0:T(8,128)(2,1)S(1)}, bf16[1,192,5120]{2,1,0:T(8,128)(2,1)}, u32[]{:S(2)}) copy-start(bf16[1,192,5120]{2,1,0:T(8,128)(2,1)} %param.6) | copy-start | bytes 5898244
  7.2 464.2 %all-reduce.2.cloned.1.call-start = ((), (), s32[]{:S(2)}) async-start(), calls=%async_computation | async-start | bytes 1310720 | tf_op jit(solution)/shard_map/psum | solution.py:37
  219.2 253.3 %copy-start.2 = (f32[32,192]{1,0:T(8,128)}, f32[32,192]{1,0:T(8,128)S(1)}, u32[]{:S(2)}) copy-start(f32[32,192]{1,0:T(8,128)S(1)} %fusion.12) | copy-start | bytes 73732
  472.5 7.2 %copy-start.1 = (f32[5120,32]{0,1:T(8,128)}, f32[5120,32]{0,1:T(8,128)S(1)}, u32[]{:S(2)}) copy-start(f32[5120,32]{0,1:T(8,128)S(1)} %broadcast_multiply_fusion) | copy-start | bytes 1966084
Sparse Core Ops, SparseCore 0:
  224.7 246.6 all-reduce.1
where the time goes:
time: 487 us
  waiting for transfers between devices  247 us (51%)
  blocking collectives  191 us (39%)
  matrix products  19.9 us (4%)
  other arithmetic  14.5 us (3%)
  between operations  14.1 us (3%)
    psum x1, waiting for transfers between devices, local(): right_total = lax.psum(right_local, ('dp', 'mp'))  247 us
    psum x1, blocking collectives, local(): left_sum = lax.psum(left_local, 'dp')  119 us
    psum x2, blocking collectives, local(): gram_matrix = lax.psum(local_gram(left_factor), 'mp')  72.1 us
  transfers between devices with their start and end apart: 1, of which 1 were waited for; matrix products, arithmetic and copies ran while one was open for 0% of the time, Pallas kernels for 0%

commit v1 on v0

v1 whole, which is shorter than its diff:
```python
import functools

import jax
import jax.numpy as jnp
from jax import lax
from jax.experimental import pallas as pl
from jax.experimental.pallas import tpu as pltpu
from jax.sharding import PartitionSpec as P

MESH = pl.DeviceIdType.MESH
F32, BF16 = jnp.float32, jnp.bfloat16
HIGHEST = lax.Precision.HIGHEST

ROWS, COLS, RANK = 192, 5120, 32
DP, MP, XS, YS = 32, 8, 4, 4
PARTS = 8
WIDE = COLS // PARTS
TILES = (RANK // 8) * (WIDE // 128)
ROW_TILES = 8


def split(value, parts):
    out = []
    for _ in range(parts):
        piece = value.astype(BF16)
        out.append(piece)
        value = value - piece.astype(F32)
    return out


def dot(a, b):
    return jnp.dot(a, b, preferred_element_type=F32)


def full_dot(a, b, dims=((1,), (0,))):
    return lax.dot_general(a, b, (dims, ((), ())), precision=HIGHEST, preferred_element_type=F32)


def inverse_cholesky(gram):
    row_id = lax.broadcasted_iota(jnp.int32, (RANK, 128), 0)
    lane_id = lax.broadcasted_iota(jnp.int32, (RANK, 128), 1)
    table = jnp.concatenate([gram, jnp.zeros((RANK, 128 - RANK), F32)], axis=1)
    table = table + jnp.where(lane_id == row_id + RANK, 1.0, 0.0)
    for j in range(RANK - 1):
        row = table[j : j + 1, :] / table[j : j + 1, j : j + 1]
        column = jnp.where(row_id > j, table[:, j : j + 1], 0.0)
        table = table - column * row
    pivots = jnp.sum(jnp.where(lane_id == row_id, table, 0.0), axis=1, keepdims=True)
    return table[:, RANK : 2 * RANK] / jnp.sqrt(pivots)


def pack(gram):
    return jnp.concatenate([gram[8 * s : 8 * s + 8, :] for s in range(4)], axis=1)


def unpack(tile):
    return jnp.concatenate([tile[:, 32 * s : 32 * s + 32] for s in range(4)], axis=0)


def exchange(
    g_hbm, e_hbm, seed_hbm, right_ref, mix_ref, left_ref,
    g_buf, e_buf, seed_buf, start, merged,
    left_tiles, left_in, left_all,
    gram_in, gram_in2,
    core_out, core_in, own, x_in, sum_tiles, dp_in, full,
    load_sem, seed_sem,
    lt_send, lt_recv, la_send, la_recv, gr_send, gr_recv,
    core_send, core_recv, x_send, x_recv, dp_send, dp_recv, dg_send, dg_recv,
    ax_send, ax_recv, ac_send, ac_recv,
):
    me = lax.axis_index("dp")
    mp = lax.axis_index("mp")
    z, y = me // YS, me % YS
    x, core = mp // 2, mp % 2
    sibling = (me, x * 2 + 1 - core)

    seed_copy = pltpu.make_async_copy(seed_hbm, seed_buf, seed_sem)
    seed_copy.start()
    loads = []
    for i in range(PARTS):
        columns = pl.ds(i * WIDE, WIDE)
        pair = (
            pltpu.make_async_copy(g_hbm.at[:, columns], g_buf.at[i], load_sem.at[0, i]),
            pltpu.make_async_copy(e_hbm.at[:, columns], e_buf.at[i], load_sem.at[1, i]),
        )
        for copy in pair:
            copy.start()
        loads.append(pair)

    barrier = pltpu.get_barrier_semaphore()

    @pl.loop(1, DP)
    def _(k):
        pl.semaphore_signal(barrier, inc=1, device_id=(lax.rem(me + k, DP), mp), device_id_type=MESH)

    @pl.loop(1, MP)
    def _(k):
        pl.semaphore_signal(barrier, inc=1, device_id=(me, lax.rem(mp + k, MP)), device_id_type=MESH)

    seed_copy.wait()
    seeds = seed_buf[...].astype(F32) * (1.0 / 1024.0)
    less = seeds - seeds[0:1, :]
    shorter = jnp.sum(less * less, axis=1, keepdims=True) < jnp.sum(seeds * seeds, axis=1, keepdims=True)
    first = lax.broadcasted_iota(jnp.int32, (RANK, 1), 0) == 0
    take = jnp.where(jnp.logical_and(shorter, jnp.logical_not(first)), 1.0, 0.0)
    seeds = seeds - take * seeds[0:1, :]
    high, low = split(seeds, 2)
    blank = jnp.zeros((64, WIDE), BF16)
    for i in range(PARTS):
        columns = slice(i * WIDE, (i + 1) * WIDE)
        start[i] = jnp.concatenate([high[:, columns], low[:, columns], blank], axis=0)

    total = jnp.zeros((2 * ROWS, 128), F32)
    for i in range(PARTS):
        for copy in loads[i]:
            copy.wait()
        both = g_buf[i].astype(F32) + e_buf[i]
        upper, lower = split(both, 2)
        merged[i, 0:ROWS, :] = upper
        merged[i, ROWS : 2 * ROWS, :] = lower
        total = total + lax.dot_general(
            merged[i], start[i], (((1,), (1,)), ((), ())), preferred_element_type=F32
        )
    left = total[0:ROWS] + total[ROWS : 2 * ROWS]
    turned = jnp.transpose(jnp.concatenate([left, jnp.zeros((64, 128), F32)], axis=0))
    left = (turned[0:RANK] + turned[RANK : 2 * RANK]) * 1.024
    for t in range(2):
        for s in range(4):
            left_tiles[4 * t + s] = left[8 * s : 8 * s + 8, 128 * t : 128 * t + 128]

    pl.semaphore_wait(barrier, DP + MP - 2)

    def remote(src, dst, send, recv, device):
        return pltpu.make_async_remote_copy(
            src_ref=src, dst_ref=dst, send_sem=send, recv_sem=recv, device_id=device, device_id_type=MESH
        )

    def wait_bytes(ref, sem):
        pltpu.make_async_copy(ref, ref, sem).wait()

    left_owner = y == lax.rem(z, YS)

    @pl.loop(0, ROW_TILES)
    def _(k):
        tile = lax.rem(z + k, ROW_TILES)
        owner = tile * YS + lax.rem(tile, YS)

        @pl.when(owner != me)
        def _():
            remote(left_tiles.at[tile], left_in.at[me], lt_send, lt_recv, (owner, mp)).start()

    @pl.when(left_owner)
    def _():
        left_in[me] = left_tiles[z]
        wait_bytes(left_in.at[pl.ds(0, DP - 1)], lt_recv)
        left_all[z] = jnp.sum(left_in[...], axis=0)

        @pl.loop(1, DP)
        def _(k):
            remote(left_all.at[z], left_all.at[z], la_send, la_recv, (lax.rem(me + k, DP), mp)).start()

        wait_bytes(left_all.at[pl.ds(0, ROW_TILES - 1)], la_recv)

    @pl.when(jnp.logical_not(left_owner))
    def _():
        wait_bytes(left_all.at[pl.ds(0, ROW_TILES)], la_recv)

    left0 = jnp.concatenate(
        [jnp.concatenate([left_all[4 * t + s] for s in range(4)], axis=0) for t in range(2)], axis=1
    )

    def send_gram(slots, which, value):
        slots[mp] = pack(full_dot(value, value, ((1,), (1,))))

        @pl.loop(1, MP)
        def _(k):
            remote(
                slots.at[mp], slots.at[mp], gr_send.at[which], gr_recv.at[which], (me, lax.rem(mp + k, MP))
            ).start()

    def take_gram(slots, which):
        wait_bytes(slots.at[pl.ds(0, MP - 1)], gr_recv.at[which])
        return unpack(jnp.sum(slots[...], axis=0))

    send_gram(gram_in, 0, left0)

    pieces = jnp.concatenate(split(left0[:, 0:ROWS], 3), axis=0)

    def right_part(part):
        one = dot(pieces, merged[part, 0:ROWS, :])
        two = dot(pieces[0 : 2 * RANK], merged[part, ROWS : 2 * ROWS, :])
        return (one[0:32] + (one[32:64] + two[0:32])) + (one[64:96] + two[32:64])

    order = (2, 1, 3, 0)
    for k in order:
        core_out[k] = right_part((1 - core) * XS + lax.rem(x + k, XS))
        remote(core_out.at[k], core_in.at[k], core_send, core_recv.at[k], sibling).start()
    for k in order:
        own[k] = right_part(core * XS + lax.rem(x + k, XS))
    for k in order:
        wait_bytes(core_in.at[k], core_recv.at[k])
        own[k] = own[k] + core_in[k]
        if k:
            target = (me, lax.rem(x + k, XS) * 2 + core)
            remote(own.at[k], x_in.at[k - 1], x_send, x_recv.at[k - 1], target).start()

    inverse1 = inverse_cholesky(take_gram(gram_in, 0))
    left1 = full_dot(inverse1, left0)
    send_gram(gram_in2, 1, left1)

    for k in range(1, XS):
        wait_bytes(x_in.at[k - 1], x_recv.at[k - 1])
    sums = (own[0] + x_in[0]) + (x_in[1] + x_in[2])
    for t in range(WIDE // 128):
        for s in range(4):
            sum_tiles[4 * t + s] = sums[8 * s : 8 * s + 8, 128 * t : 128 * t + 128]

    mine = core * XS + x
    owns = me < TILES

    @pl.loop(1, DP)
    def _(k):
        owner = lax.rem(me + k, DP)

        @pl.when(owner < TILES)
        def _():
            remote(sum_tiles.at[owner], dp_in.at[me], dp_send, dp_recv, (owner, mp)).start()

    @pl.when(owns)
    def _():
        dp_in[me] = sum_tiles[me]
        wait_bytes(dp_in.at[pl.ds(0, DP - 1)], dp_recv)
        full[mine, me] = jnp.sum(dp_in[...], axis=0)

        @pl.loop(1, DP)
        def _(k):
            remote(
                full.at[mine, me], full.at[mine, me], dg_send, dg_recv, (lax.rem(me + k, DP), mp)
            ).start()

        wait_bytes(full.at[0, pl.ds(0, TILES - 1)], dg_recv)

    @pl.when(jnp.logical_not(owns))
    def _():
        wait_bytes(full.at[0], dg_recv)

    for k in range(1, XS):
        target = (me, lax.rem(x + k, XS) * 2 + core)
        remote(full.at[mine], full.at[mine], ax_send, ax_recv.at[k - 1], target).start()
    remote(full.at[mine], full.at[mine], ac_send, ac_recv.at[0], sibling).start()

    inverse2 = inverse_cholesky(take_gram(gram_in2, 1))
    left_ref[...] = full_dot(inverse2, left1)[:, 0:ROWS]
    mix_ref[...] = full_dot(inverse2, inverse1)

    for k in (1, 3, 2):
        got = core * XS + lax.rem(x + XS - k, XS)
        wait_bytes(full.at[0], ax_recv.at[k - 1])
        remote(full.at[got], full.at[got], ac_send, ac_recv.at[k], sibling).start()
    for k in range(XS):
        wait_bytes(full.at[0], ac_recv.at[k])
    right_ref[...] = full[...]

    @pl.when(left_owner)
    def _():
        wait_bytes(left_in.at[pl.ds(0, ROW_TILES - 1)], lt_send)
        wait_bytes(left_in.at[pl.ds(0, DP - 1)], la_send)

    @pl.when(jnp.logical_not(left_owner))
    def _():
        wait_bytes(left_in.at[pl.ds(0, ROW_TILES)], lt_send)

    for which in range(2):
        wait_bytes(left_in.at[pl.ds(0, MP - 1)], gr_send.at[which])

    @pl.when(owns)
    def _():
        wait_bytes(dp_in.at[pl.ds(0, TILES - 1)], dp_send)
        wait_bytes(dp_in.at[pl.ds(0, DP - 1)], dg_send)

    @pl.when(jnp.logical_not(owns))
    def _():
        wait_bytes(dp_in.at[pl.ds(0, TILES)], dp_send)

    wait_bytes(core_out, core_send)
    wait_bytes(x_in, x_send)
    wait_bytes(x_in, ax_send)
    wait_bytes(core_out, ac_send)


def run_exchange(gradients, errors, seeds):
    hbm = pl.BlockSpec(memory_space=pl.ANY)
    vmem = pl.BlockSpec(memory_space=pltpu.VMEM)
    dma = pltpu.SemaphoreType.DMA
    return pl.pallas_call(
        exchange,
        out_shape=(
            jax.ShapeDtypeStruct((PARTS, TILES, 8, 128), F32),
            jax.ShapeDtypeStruct((RANK, RANK), F32),
            jax.ShapeDtypeStruct((RANK, ROWS), F32),
        ),
        in_specs=[hbm, hbm, hbm],
        out_specs=(vmem, vmem, vmem),
        scratch_shapes=[
            pltpu.VMEM((PARTS, ROWS, WIDE), BF16),
            pltpu.VMEM((PARTS, ROWS, WIDE), F32),
            pltpu.VMEM((RANK, COLS), jnp.int32),
            pltpu.VMEM((PARTS, 128, WIDE), BF16),
            pltpu.VMEM((PARTS, 2 * ROWS, WIDE), BF16),
            pltpu.VMEM((ROW_TILES, 8, 128), F32),
            pltpu.VMEM((DP, 8, 128), F32),
            pltpu.VMEM((ROW_TILES, 8, 128), F32),
            pltpu.VMEM((MP, 8, 128), F32),
            pltpu.VMEM((MP, 8, 128), F32),
            pltpu.VMEM((XS, RANK, WIDE), F32),
            pltpu.VMEM((XS, RANK, WIDE), F32),
            pltpu.VMEM((XS, RANK, WIDE), F32),
            pltpu.VMEM((XS - 1, RANK, WIDE), F32),
            pltpu.VMEM((TILES, 8, 128), F32),
            pltpu.VMEM((DP, 8, 128), F32),
            pltpu.VMEM((PARTS, TILES, 8, 128), F32),
            dma((2, PARTS)),
            dma,
            dma, dma, dma, dma, dma((2,)), dma((2,)),
            dma, dma((XS,)), dma, dma((XS - 1,)), dma, dma, dma, dma,
            dma, dma((XS - 1,)), dma, dma((XS,)),
        ],
        compiler_params=pltpu.CompilerParams(
            collective_id=0, has_side_effects=True, vmem_limit_bytes=40 * 1024 * 1024
        ),
        cost_estimate=pl.CostEstimate(flops=10**9, bytes_accessed=8 * 10**6, transcendentals=0),
        name="exchange",
    )(gradients, errors, seeds)


def finish(g_ref, e_ref, sums_ref, mix_ref, left_ref, new_ref, update_ref, right_ref, left_out):
    def stack_left(value):
        h, m, l = [p.astype(F32) for p in split(value, 3)]
        return jnp.concatenate([h, h, m, m, h, l], axis=0)

    def stack_right(value):
        h, m, l = split(value, 3)
        return jnp.concatenate([h, m, h, m, l, h], axis=0)

    mix = mix_ref[...]
    mix_t = jnp.concatenate([jnp.transpose(jnp.pad(mix, ((0, 96), (0, 96))))[0:32]], axis=0)
    mix_wide = jnp.transpose(stack_left(mix_t)).astype(BF16)
    left = left_ref[...]
    left_wide = jnp.transpose(stack_left(left)).astype(BF16)
    for part in range(sums_ref.shape[0]):
        columns = slice(part * WIDE, (part + 1) * WIDE)
        sums = jnp.concatenate(
            [
                jnp.concatenate([sums_ref[part, 4 * t + s] for s in range(4)], axis=0)
                for t in range(WIDE // 128)
            ],
            axis=1,
        )
        right = dot(mix_wide, stack_right(sums))[0:RANK] * (1.0 / DP)
        right_ref[:, columns] = right
        approx = dot(left_wide, stack_right(right))
        update_ref[:, columns] = approx.astype(BF16)
        new_ref[:, columns] = (g_ref[:, columns].astype(F32) + e_ref[:, columns]) - approx
    left_out[...] = left


def run_finish(gradients, errors, sums, mix, left):
    parts = 2
    wide = parts * WIDE
    columns = lambda rows: pl.BlockSpec((rows, wide), lambda i: (0, i))
    whole = lambda *shape: pl.BlockSpec(shape, lambda i: (0,) * len(shape))
    return pl.pallas_call(
        finish,
        grid=(PARTS // parts,),
        out_shape=(
            jax.ShapeDtypeStruct((ROWS, COLS), F32),
            jax.ShapeDtypeStruct((ROWS, COLS), BF16),
            jax.ShapeDtypeStruct((RANK, COLS), F32),
            jax.ShapeDtypeStruct((RANK, ROWS), F32),
        ),
        in_specs=[
            columns(ROWS),
            columns(ROWS),
            pl.BlockSpec((parts, TILES, 8, 128), lambda i: (i, 0, 0, 0)),
            whole(RANK, RANK),
            whole(RANK, ROWS),
        ],
        out_specs=(columns(ROWS), columns(ROWS), columns(RANK), whole(RANK, ROWS)),
        compiler_params=pltpu.CompilerParams(vmem_limit_bytes=40 * 1024 * 1024),
        cost_estimate=pl.CostEstimate(flops=10**9, bytes_accessed=14 * 10**6, transcendentals=0),
        name="finish",
    )(gradients, errors, sums, mix, left)


def local(gradients, errors, seed_table):
    sums, mix, left = run_exchange(gradients[0], errors[0], seed_table.T)
    new_errors, update, right, left = run_finish(gradients[0], errors[0], sums, mix, left)
    return (new_errors[None], update, right.T, left.T)


def solution(mesh):
    in_specs = (P("dp", "mp", None), P("dp", "mp", None), P())
    out_specs = (P("dp", "mp", None), P("mp", None), P(), P("mp", None))
    return jax.shard_map(local, mesh=mesh, in_specs=in_specs, out_specs=out_specs, check_vma=False)
```

time: 487 us -> 62.9 us (0.13)
  waiting for transfers between devices: 247 us -> 0 us
  blocking collectives: 191 us -> 0 us
  Pallas kernels: 0 us -> 57.3 us
  matrix products: 19.9 us -> 0 us
  other arithmetic: 14.5 us -> 0 us
  between operations: 14.1 us -> 0.65 us
    psum x1 -> x0, waiting for transfers between devices: 247 us -> none  [local(): right_total = lax.psum(right_local, ('dp', 'mp'))]
    psum x3 -> x0, blocking collectives: 191 us -> none  [the longest x1 119 us: local(): left_sum = lax.psum(left_local, 'dp')]
    pallas_call x0 -> x2, Pallas kernels: none -> 57.3 us  [the longest x1 52.4 us: run_exchange(): pl.pallas_call(exchange, out_shape=(jax.ShapeDtypeStruct((PARTS, TILES, 8...]
    dot_general x5 -> x0, matrix products: 19.4 us -> none  [the longest x1 7.21 us: local(): jnp.dot(left_factor, right_factor.T, precision=lax.Precision.HIGHEST, pre...]
    another operation x10 -> x0, other arithmetic: 13.4 us -> none  [the longest x6 7.19 us: cholesky_step(): lower = jnp.linalg.cholesky(gram_matrix)]
  transfers between devices with their start and end apart: 1 -> 0, of which waited for: 1 -> 0; matrix products, arithmetic and copies ran while one was open for 0% -> 0% of each run, Pallas kernels for 0% -> 0%
where the time goes in v1:
time: 62.9 us; the launch traced here: 62.7 us
  Pallas kernels  57.3 us (91%)
  local copies, waits for them, and re-layouts  4.74 us (8%)
  between operations  0.65 us (1%)
    pallas_call x1, Pallas kernels, run_exchange(): pl.pallas_call(exchange, out_shape=(jax.ShapeDtypeStruct((PARTS, TILES, 8...  52.4 us
    pallas_call x1, Pallas kernels, run_finish(): pl.pallas_call(finish, grid=(PARTS // parts,), out_shape=(jax.ShapeDtypeS...  4.89 us
    unnamed x6, local copies, waits for them, and re-layouts  4.74 us

profile of v1, /device:TPU:1, one launch (start us, length us, event | category | flops | bytes accessed | tf_op | source)
XLA Modules:
  0.0 62.7 jit_solution(7629568085378519773)
XLA Ops:
  0.6 0.0 copy-start
  0.6 2.1 %copy-done = f32[1,192,5120]{2,1,0:T(8,128)S(1)} copy-done((f32[1,192,5120]{2,1,0:T(8,128)S(1)}, f32[1,192,5120]{2,1,0:T(8,128)}, u32[]{:S(2)}) %copy-start) | copy-done | bytes 3932184
  2.7 0.0 copy-start.1
  2.7 1.5 %copy-done.1 = bf16[1,192,5120]{2,1,0:T(8,128)(2,1)S(1)} copy-done((bf16[1,192,5120]{2,1,0:T(8,128)(2,1)S(1)}, bf16[1,192,5120]{2,1,0:T(8,128)(2,1)}, u32[]{:S(2)}) %copy-start.1) | copy-done | bytes 1966104
  4.3 0.0 copy-start.2
  4.3 1.1 %copy-done.2 = s32[5120,32]{0,1:T(8,128)S(1)} copy-done((s32[5120,32]{0,1:T(8,128)S(1)}, s32[5120,32]{0,1:T(8,128)}, u32[]{:S(2)}) %copy-start.2) | copy-done | bytes 655384
  5.4 52.4 %exchange.1 = (f32[8,20,8,128]{3,2,1,0:T(8,128)S(1)}, f32[32,32]{1,0:T(8,128)S(1)}, f32[32,192]{1,0:T(8,128)S(1)}) custom-call(bf16[192,5120]{1,0:T(8,128)(2,1)S(1)} %bitcast.8, f32[192,5120]{1,0:T(8,128)S(1)} %bitcast.6, s32[32,5120]{1,0:T(8,128)S(1)} %bitcast.10), custom_call_target="tpu_custom_call" | custom-call | flops 1000000000 | bytes 8000000 | tf_op jit(solution)/shard_map/exchange/pallas_call | solution.py:295
  57.8 4.9 %finish.1 = (f32[192,5120]{1,0:T(8,128)}, bf16[192,5120]{1,0:T(8,128)(2,1)}, f32[32,5120]{1,0:T(8,128)}, f32[32,192]{1,0:T(8,128)}) custom-call(bf16[192,5120]{1,0:T(8,128)(2,1)S(1)} %bitcast.9, f32[192,5120]{1,0:T(8,128)S(1)} %bitcast.7, f32[8,20,8,128]{3,2,1,0:T(8,128)S(1)} %get-tuple-element.11.sums_ref, f32[32,32]{1,0:T(8,128)S(1)} %get-tuple-element.12.mix_ref, ...), custom_call_target="tpu_custom_call" | custom-call | flops 1000000000 | bytes 14000000 | tf_op jit(solution)/shard_map/finish/pallas_call | solution.py:372
Async XLA Ops:
  0.6 2.1 %copy-start = (f32[1,192,5120]{2,1,0:T(8,128)S(1)}, f32[1,192,5120]{2,1,0:T(8,128)}, u32[]{:S(2)}) copy-start(f32[1,192,5120]{2,1,0:T(8,128)} %param.4) | copy-start | bytes 11796484
  2.7 1.5 %copy-start.1 = (bf16[1,192,5120]{2,1,0:T(8,128)(2,1)S(1)}, bf16[1,192,5120]{2,1,0:T(8,128)(2,1)}, u32[]{:S(2)}) copy-start(bf16[1,192,5120]{2,1,0:T(8,128)(2,1)} %param.3) | copy-start | bytes 5898244
  4.3 1.1 %copy-start.2 = (s32[5120,32]{0,1:T(8,128)S(1)}, s32[5120,32]{0,1:T(8,128)}, u32[]{:S(2)}) copy-start(s32[5120,32]{0,1:T(8,128)} %param.5) | copy-start | bytes 1966084

commit v2 on v1

v2 whole, which is shorter than its diff:
```python
import jax
import jax.numpy as jnp
from jax import lax
from jax.experimental import pallas as pl
from jax.experimental.pallas import tpu as pltpu
from jax.sharding import PartitionSpec as P

MESH = pl.DeviceIdType.MESH
F32, BF16 = jnp.float32, jnp.bfloat16
HIGHEST = lax.Precision.HIGHEST

ROWS, COLS, RANK = 192, 5120, 32
DP, MP, XS, YS = 32, 8, 4, 4
PARTS = 8
WIDE = COLS // PARTS
ROW_TILES = 8


def split(value, parts):
    out = []
    for _ in range(parts):
        piece = value.astype(BF16)
        out.append(piece)
        value = value - piece.astype(F32)
    return out


def dot(a, b):
    return jnp.dot(a, b, preferred_element_type=F32)


def full_dot(a, b, dims=((1,), (0,))):
    return lax.dot_general(a, b, (dims, ((), ())), precision=HIGHEST, preferred_element_type=F32)


def inverse_cholesky(gram):
    row_id = lax.broadcasted_iota(jnp.int32, (RANK, 128), 0)
    lane_id = lax.broadcasted_iota(jnp.int32, (RANK, 128), 1)
    table = jnp.concatenate([gram, jnp.zeros((RANK, 128 - RANK), F32)], axis=1)
    table = table + jnp.where(lane_id == row_id + RANK, 1.0, 0.0)
    for j in range(RANK - 1):
        row = table[j : j + 1, :] / table[j : j + 1, j : j + 1]
        column = jnp.where(row_id > j, table[:, j : j + 1], 0.0)
        table = table - column * row
    pivots = jnp.sum(jnp.where(lane_id == row_id, table, 0.0), axis=1, keepdims=True)
    return table[:, RANK : 2 * RANK] / jnp.sqrt(pivots)


def pack(gram):
    return jnp.concatenate([gram[8 * s : 8 * s + 8, :] for s in range(4)], axis=1)


def unpack(tile):
    return jnp.concatenate([tile[:, 32 * s : 32 * s + 32] for s in range(4)], axis=0)


def stack_left(value):
    h, m, l = [p.astype(F32) for p in split(value, 3)]
    return jnp.concatenate([h, h, m, m, h, l], axis=0)


def stack_right(value):
    h, m, l = split(value, 3)
    return jnp.concatenate([h, m, h, m, l, h], axis=0)


def exchange(
    g_hbm, e_hbm, seed_hbm, both_ref, right_ref, wide_ref, left_ref,
    g_buf, e_buf, seed_buf, start, merged,
    left_tiles, left_in, left_all,
    gram_in, gram_in2,
    core_out, core_in, own, xy_in, z_in, full,
    load_sem, seed_sem,
    lt_send, lt_recv, la_send, la_recv, gr_send, gr_recv,
    core_send, core_recv, xy_send, xy_recv, z_send, z_recv,
    ag_send, ag_recv, ac_send, ac_recv,
):
    me = lax.axis_index("dp")
    mp = lax.axis_index("mp")
    z, y = me // YS, me % YS
    x, core = mp // 2, mp % 2
    sibling = (me, x * 2 + 1 - core)

    def plane(kx, ky):
        return (z * YS + lax.rem(y + ky, YS), lax.rem(x + kx, XS) * 2 + core)

    seed_copy = pltpu.make_async_copy(seed_hbm, seed_buf, seed_sem)
    seed_copy.start()
    loads = []
    for i in range(PARTS):
        columns = pl.ds(i * WIDE, WIDE)
        pair = (
            pltpu.make_async_copy(g_hbm.at[:, columns], g_buf.at[i], load_sem.at[0, i]),
            pltpu.make_async_copy(e_hbm.at[:, columns], e_buf.at[i], load_sem.at[1, i]),
        )
        for copy in pair:
            copy.start()
        loads.append(pair)

    barrier = pltpu.get_barrier_semaphore()

    @pl.loop(1, DP)
    def _(k):
        pl.semaphore_signal(barrier, inc=1, device_id=(lax.rem(me + k, DP), mp), device_id_type=MESH)

    @pl.loop(1, MP)
    def _(k):
        pl.semaphore_signal(barrier, inc=1, device_id=(me, lax.rem(mp + k, MP)), device_id_type=MESH)

    for kx in range(1, XS):
        for ky in range(1, YS):
            pl.semaphore_signal(barrier, inc=1, device_id=plane(kx, ky), device_id_type=MESH)

    seed_copy.wait()
    seeds = seed_buf[...].astype(F32) * (1.0 / 1024.0)
    less = seeds - seeds[0:1, :]
    shorter = jnp.sum(less * less, axis=1, keepdims=True) < jnp.sum(seeds * seeds, axis=1, keepdims=True)
    first = lax.broadcasted_iota(jnp.int32, (RANK, 1), 0) == 0
    take = jnp.where(jnp.logical_and(shorter, jnp.logical_not(first)), 1.0, 0.0)
    seeds = seeds - take * seeds[0:1, :]
    high, low = split(seeds, 2)
    blank = jnp.zeros((64, WIDE), BF16)
    for i in range(PARTS):
        columns = slice(i * WIDE, (i + 1) * WIDE)
        start[i] = jnp.concatenate([high[:, columns], low[:, columns], blank], axis=0)

    total = jnp.zeros((2 * ROWS, 128), F32)
    for i in range(PARTS):
        for copy in loads[i]:
            copy.wait()
        both = g_buf[i].astype(F32) + e_buf[i]
        both_ref[i] = both
        upper, lower = split(both, 2)
        merged[i, 0:ROWS, :] = upper
        merged[i, ROWS : 2 * ROWS, :] = lower
        total = total + lax.dot_general(
            merged[i], start[i], (((1,), (1,)), ((), ())), preferred_element_type=F32
        )
    left = total[0:ROWS] + total[ROWS : 2 * ROWS]
    turned = jnp.transpose(jnp.concatenate([left, jnp.zeros((64, 128), F32)], axis=0))
    left = (turned[0:RANK] + turned[RANK : 2 * RANK]) * 1.024
    for t in range(2):
        for s in range(4):
            left_tiles[4 * t + s] = left[8 * s : 8 * s + 8, 128 * t : 128 * t + 128]

    pl.semaphore_wait(barrier, DP + MP - 2 + (XS - 1) * (YS - 1))

    def remote(src, dst, send, recv, device):
        return pltpu.make_async_remote_copy(
            src_ref=src, dst_ref=dst, send_sem=send, recv_sem=recv, device_id=device, device_id_type=MESH
        )

    def wait_bytes(ref, sem):
        pltpu.make_async_copy(ref, ref, sem).wait()

    left_owner = y == lax.rem(z, YS)

    @pl.loop(0, ROW_TILES)
    def _(k):
        tile = lax.rem(z + k, ROW_TILES)
        owner = tile * YS + lax.rem(tile, YS)

        @pl.when(owner != me)
        def _():
            remote(left_tiles.at[tile], left_in.at[me], lt_send, lt_recv, (owner, mp)).start()

    @pl.when(left_owner)
    def _():
        left_in[me] = left_tiles[z]
        wait_bytes(left_in.at[pl.ds(0, DP - 1)], lt_recv)
        left_all[z] = jnp.sum(left_in[...], axis=0)

        @pl.loop(1, DP)
        def _(k):
            remote(left_all.at[z], left_all.at[z], la_send, la_recv, (lax.rem(me + k, DP), mp)).start()

        wait_bytes(left_all.at[pl.ds(0, ROW_TILES - 1)], la_recv)

    @pl.when(jnp.logical_not(left_owner))
    def _():
        wait_bytes(left_all.at[pl.ds(0, ROW_TILES)], la_recv)

    left0 = jnp.concatenate(
        [jnp.concatenate([left_all[4 * t + s] for s in range(4)], axis=0) for t in range(2)], axis=1
    )

    def send_gram(slots, which, value):
        slots[mp] = pack(full_dot(value, value, ((1,), (1,))))

        @pl.loop(1, MP)
        def _(k):
            remote(
                slots.at[mp], slots.at[mp], gr_send.at[which], gr_recv.at[which], (me, lax.rem(mp + k, MP))
            ).start()

    def take_gram(slots, which):
        wait_bytes(slots.at[pl.ds(0, MP - 1)], gr_recv.at[which])
        return unpack(jnp.sum(slots[...], axis=0))

    send_gram(gram_in, 0, left0)

    pieces = jnp.concatenate(split(left0[:, 0:ROWS], 3), axis=0)

    def right_part(into, part):
        one = dot(pieces, merged[part, 0:ROWS, :])
        two = dot(pieces[0 : 2 * RANK], merged[part, ROWS : 2 * ROWS, :])
        value = (one[0:32] + (one[32:64] + two[0:32])) + (one[64:96] + two[32:64])
        for s in range(YS):
            into[s] = value[8 * s : 8 * s + 8]

    order = (2, 1, 3, 0)
    for k in order:
        right_part(core_out.at[k], (1 - core) * XS + lax.rem(x + k, XS))
        remote(core_out.at[k], core_in.at[k], core_send, core_recv.at[k], sibling).start()
    for k in order:
        right_part(own.at[k], core * XS + lax.rem(x + k, XS))

    for kx in order:
        wait_bytes(core_in.at[kx], core_recv.at[kx])
        own[kx] = own[kx] + core_in[kx]
        for ky in (2, 1, 3, 0):
            if kx or ky:
                slot = kx * YS + ky - 1
                remote(
                    own.at[kx, lax.rem(y + ky, YS)], xy_in.at[slot], xy_send, xy_recv, plane(kx, ky)
                ).start()

    inverse1 = inverse_cholesky(take_gram(gram_in, 0))
    left1 = full_dot(inverse1, left0)
    send_gram(gram_in2, 1, left1)

    wait_bytes(xy_in, xy_recv)
    z_in[z] = own[0, y] + jnp.sum(xy_in[...], axis=0)

    @pl.loop(1, ROW_TILES)
    def _(k):
        remote(z_in.at[z], z_in.at[z], z_send, z_recv, (lax.rem(z + k, 8) * YS + y, mp)).start()

    inverse2 = inverse_cholesky(take_gram(gram_in2, 1))
    left2 = full_dot(inverse2, left1)[:, 0:ROWS]
    left_ref[...] = left2
    wide_ref[...] = jnp.transpose(stack_left(left2)).astype(BF16)
    mix = full_dot(inverse2, inverse1)
    mix = jnp.transpose(jnp.pad(mix, ((0, 96), (0, 96))))[0:RANK]
    mix = jnp.transpose(stack_left(mix)).astype(BF16)[0:RANK]

    mine = core * XS + x
    wait_bytes(z_in.at[pl.ds(0, 7)], z_recv)
    full[mine, y] = jnp.sum(z_in[...], axis=0)
    for kx in order:
        for ky in (2, 1, 3, 0):
            if kx or ky:
                remote(full.at[mine, y], full.at[mine, y], ag_send, ag_recv.at[kx], plane(kx, ky)).start()

    def right_of(part):
        sums = jnp.concatenate([full[part, s] for s in range(4)], axis=0)
        right_ref[part] = dot(mix, stack_right(sums)) * (1.0 / DP)

    for kx in (0, 1, 3, 2):
        got = core * XS + lax.rem(x + XS - kx, XS)
        wait_bytes(full.at[0, pl.ds(0, YS if kx else YS - 1)], ag_recv.at[kx])
        remote(full.at[got], full.at[got], ac_send, ac_recv.at[kx], sibling).start()
        right_of(got)
    for kx in (0, 1, 3, 2):
        wait_bytes(full.at[0], ac_recv.at[kx])
        right_of((1 - core) * XS + lax.rem(x + XS - kx, XS))

    @pl.when(left_owner)
    def _():
        wait_bytes(left_in.at[pl.ds(0, ROW_TILES - 1)], lt_send)
        wait_bytes(left_in.at[pl.ds(0, DP - 1)], la_send)

    @pl.when(jnp.logical_not(left_owner))
    def _():
        wait_bytes(left_in.at[pl.ds(0, ROW_TILES)], lt_send)

    for which in range(2):
        wait_bytes(left_in.at[pl.ds(0, MP - 1)], gr_send.at[which])
    wait_bytes(core_out, core_send)
    wait_bytes(xy_in, xy_send)
    wait_bytes(z_in.at[pl.ds(0, 7)], z_send)
    wait_bytes(xy_in, ag_send)
    wait_bytes(core_out, ac_send)


def run_exchange(gradients, errors, seeds):
    hbm = pl.BlockSpec(memory_space=pltpu.HBM)
    vmem = pl.BlockSpec(memory_space=pltpu.VMEM)
    dma = pltpu.SemaphoreType.DMA
    return pl.pallas_call(
        exchange,
        out_shape=(
            jax.ShapeDtypeStruct((PARTS, ROWS, WIDE), F32),
            jax.ShapeDtypeStruct((PARTS, RANK, WIDE), F32),
            jax.ShapeDtypeStruct((ROWS, 6 * RANK), BF16),
            jax.ShapeDtypeStruct((RANK, ROWS), F32),
        ),
        in_specs=[hbm, hbm, hbm],
        out_specs=(vmem,) * 4,
        scratch_shapes=[
            pltpu.VMEM((PARTS, ROWS, WIDE), BF16),
            pltpu.VMEM((PARTS, ROWS, WIDE), F32),
            pltpu.VMEM((RANK, COLS), jnp.int32),
            pltpu.VMEM((PARTS, 128, WIDE), BF16),
            pltpu.VMEM((PARTS, 2 * ROWS, WIDE), BF16),
            pltpu.VMEM((ROW_TILES, 8, 128), F32),
            pltpu.VMEM((DP, 8, 128), F32),
            pltpu.VMEM((ROW_TILES, 8, 128), F32),
            pltpu.VMEM((MP, 8, 128), F32),
            pltpu.VMEM((MP, 8, 128), F32),
            pltpu.VMEM((XS, YS, 8, WIDE), F32),
            pltpu.VMEM((XS, YS, 8, WIDE), F32),
            pltpu.VMEM((XS, YS, 8, WIDE), F32),
            pltpu.VMEM((XS * YS - 1, 8, WIDE), F32),
            pltpu.VMEM((DP // YS, 8, WIDE), F32),
            pltpu.VMEM((PARTS, YS, 8, WIDE), F32),
            dma((2, PARTS)),
            dma,
            dma, dma, dma, dma, dma((2,)), dma((2,)),
            dma, dma((XS,)), dma, dma, dma, dma,
            dma, dma((XS,)), dma, dma((XS,)),
        ],
        compiler_params=pltpu.CompilerParams(
            collective_id=0, has_side_effects=True, vmem_limit_bytes=40 * 1024 * 1024
        ),
        cost_estimate=pl.CostEstimate(flops=10**9, bytes_accessed=8 * 10**6, transcendentals=0),
        name="exchange",
    )(*(pltpu.with_memory_space_constraint(v, pltpu.HBM) for v in (gradients, errors, seeds)))


def finish(
    both_ref, right_ref, wide_ref, left_ref, new_hbm, update_hbm, right_hbm, left_hbm,
    new_buf, update_buf, new_sem, update_sem, right_sem, left_sem,
):
    copies = [pltpu.make_async_copy(left_ref, left_hbm, left_sem)]
    copies[0].start()
    for part in range(PARTS):
        columns = pl.ds(part * WIDE, WIDE)
        approx = dot(wide_ref[...], stack_right(right_ref[part]))
        new_buf[part] = both_ref[part] - approx
        update_buf[part] = approx.astype(BF16)
        for copy in (
            pltpu.make_async_copy(new_buf.at[part], new_hbm.at[:, columns], new_sem.at[part]),
            pltpu.make_async_copy(update_buf.at[part], update_hbm.at[:, columns], update_sem.at[part]),
            pltpu.make_async_copy(right_ref.at[part], right_hbm.at[:, columns], right_sem.at[part]),
        ):
            copy.start()
            copies.append(copy)
    for copy in copies:
        copy.wait()


def run_finish(*operands):
    hbm = pl.BlockSpec(memory_space=pltpu.HBM)
    vmem = pl.BlockSpec(memory_space=pltpu.VMEM)
    dma = pltpu.SemaphoreType.DMA
    return pl.pallas_call(
        finish,
        out_shape=(
            jax.ShapeDtypeStruct((ROWS, COLS), F32),
            jax.ShapeDtypeStruct((ROWS, COLS), BF16),
            jax.ShapeDtypeStruct((RANK, COLS), F32),
            jax.ShapeDtypeStruct((RANK, ROWS), F32),
        ),
        in_specs=[vmem] * 4,
        out_specs=(hbm,) * 4,
        scratch_shapes=[
            pltpu.VMEM((PARTS, ROWS, WIDE), F32),
            pltpu.VMEM((PARTS, ROWS, WIDE), BF16),
            dma((PARTS,)), dma((PARTS,)), dma((PARTS,)), dma,
        ],
        compiler_params=pltpu.CompilerParams(vmem_limit_bytes=40 * 1024 * 1024),
        cost_estimate=pl.CostEstimate(flops=10**9, bytes_accessed=10**7, transcendentals=0),
        name="finish",
    )(*operands)


def local(gradients, errors, seed_table):
    new_errors, update, right, left = run_finish(*run_exchange(gradients[0], errors[0], seed_table.T))
    return (new_errors[None], update, right.T, left.T)


def solution(mesh):
    in_specs = (P("dp", "mp", None), P("dp", "mp", None), P())
    out_specs = (P("dp", "mp", None), P("mp", None), P(), P("mp", None))
    return jax.shard_map(local, mesh=mesh, in_specs=in_specs, out_specs=out_specs, check_vma=False)
```

time: 62.9 us -> 53.4 us (0.85)
  local copies, waits for them, and re-layouts: 4.74 us -> 0 us
  Pallas kernels: 57.3 us -> 52.7 us
    unnamed x6 -> x0, local copies, waits for them, and re-layouts: 4.74 us -> none
    pallas_call x2, Pallas kernels: 57.3 us -> 52.7 us  [the longest x1 49.5 us: run_exchange(): pl.pallas_call(exchange, out_shape=(jax.ShapeDtypeStruct((PARTS, ROWS, WI...]
where the time goes in v2:
time: 53.4 us; the launch traced here: 53.3 us
  Pallas kernels  52.7 us (99%)
  between operations  0.64 us (1%)
    pallas_call x1, Pallas kernels, run_exchange(): pl.pallas_call(exchange, out_shape=(jax.ShapeDtypeStruct((PARTS, ROWS, WI...  49.5 us
    pallas_call x1, Pallas kernels, run_finish(): pl.pallas_call(finish, out_shape=(jax.ShapeDtypeStruct((ROWS, COLS), F32)...  3.21 us

profile of v2, /device:TPU:1, one launch (start us, length us, event | category | flops | bytes accessed | tf_op | source)
XLA Modules:
  0.0 53.3 jit_solution(5092408123487689271)
XLA Ops:
  0.6 49.5 %exchange.1 = (f32[8,192,640]{2,1,0:T(8,128)S(1)}, f32[8,32,640]{2,1,0:T(8,128)S(1)}, bf16[192,192]{1,0:T(8,128)(2,1)S(1)}, f32[32,192]{1,0:T(8,128)S(1)}) custom-call(bf16[192,5120]{1,0:T(8,128)(2,1)} %bitcast.7, f32[192,5120]{1,0:T(8,128)} %bitcast.6, s32[32,5120]{1,0:T(8,128)} %bitcast.8), custom_call_target="tpu_custom_call" | custom-call | flops 1000000000 | bytes 8000000 | tf_op jit(solution)/shard_map/exchange/pallas_call | solution.py:290
  50.1 3.2 %finish.1 = (f32[192,5120]{1,0:T(8,128)}, bf16[192,5120]{1,0:T(8,128)(2,1)}, f32[32,5120]{1,0:T(8,128)}, f32[32,192]{1,0:T(8,128)}) custom-call(f32[8,192,640]{2,1,0:T(8,128)S(1)} %get-tuple-element.12.both_ref, f32[8,32,640]{2,1,0:T(8,128)S(1)} %get-tuple-element.13.right_ref, bf16[192,192]{1,0:T(8,128)(2,1)S(1)} %get-tuple-element.14.wide_ref, ...), custom_call_target="tpu_custom_call" | custom-call | flops 1000000000 | bytes 10000000 | tf_op jit(solution)/shard_map/finish/pallas_call | solution.py:357

commit v3 on v2

--- a/solution.py
+++ b/solution.py
@@ -14,6 +14,15 @@
 PARTS = 8
 WIDE = COLS // PARTS
 ROW_TILES = 8
+STREAMS = ((0, 384), (384, 256))
+GROUPS = ((0, 1), (2, 3), (4, 5), (6,), (7,))
+ZS = DP // YS
+FAR_Z = (4, 3, 5, 2, 6, 1, 7, 0)
+FAR = (2, 1, 3, 0)
+FAR_DP = sorted(
+    ((dz, dy) for dz in range(ZS) for dy in range(YS) if dz or dy),
+    key=lambda d: -min(d[0], ZS - d[0]) - min(d[1], YS - d[1]),
+)
 
 
 def split(value, parts):
@@ -69,7 +78,8 @@
     g_buf, e_buf, seed_buf, start, merged,
     left_tiles, left_in, left_all,
     gram_in, gram_in2,
-    core_out, core_in, own, xy_in, z_in, full,
+    core_out_a, core_in_a, own_a, xy_in_a, z_in_a, full_a,
+    core_out_b, core_in_b, own_b, xy_in_b, z_in_b, full_b,
     load_sem, seed_sem,
     lt_send, lt_recv, la_send, la_recv, gr_send, gr_recv,
     core_send, core_recv, xy_send, xy_recv, z_send, z_recv,
@@ -84,8 +94,17 @@
     def plane(kx, ky):
         return (z * YS + lax.rem(y + ky, YS), lax.rem(x + kx, XS) * 2 + core)
 
+    def over_dp(dz, dy):
+        return (lax.rem(z + dz, ZS) * YS + lax.rem(y + dy, YS), mp)
+
+    barrier = pltpu.get_barrier_semaphore()
     seed_copy = pltpu.make_async_copy(seed_hbm, seed_buf, seed_sem)
     seed_copy.start()
+    peers = [over_dp(*d) for d in FAR_DP] + [plane(kx, ky) for kx in FAR[:3] for ky in FAR[:3]]
+    peers += [(me, lax.rem(mp + k, MP)) for k in range(1, MP)]
+    for peer in peers:
+        pl.semaphore_signal(barrier, inc=1, device_id=peer, device_id_type=MESH)
+
     loads = []
     for i in range(PARTS):
         columns = pl.ds(i * WIDE, WIDE)
@@ -96,20 +115,6 @@
         for copy in pair:
             copy.start()
         loads.append(pair)
-
-    barrier = pltpu.get_barrier_semaphore()
-
-    @pl.loop(1, DP)
-    def _(k):
-        pl.semaphore_signal(barrier, inc=1, device_id=(lax.rem(me + k, DP), mp), device_id_type=MESH)
-
-    @pl.loop(1, MP)
-    def _(k):
-        pl.semaphore_signal(barrier, inc=1, device_id=(me, lax.rem(mp + k, MP)), device_id_type=MESH)
-
-    for kx in range(1, XS):
-        for ky in range(1, YS):
-            pl.semaphore_signal(barrier, inc=1, device_id=plane(kx, ky), device_id_type=MESH)
 
     seed_copy.wait()
     seeds = seed_buf[...].astype(F32) * (1.0 / 1024.0)
@@ -124,18 +129,25 @@
         columns = slice(i * WIDE, (i + 1) * WIDE)
         start[i] = jnp.concatenate([high[:, columns], low[:, columns], blank], axis=0)
 
+    def product(group):
+        a = jnp.concatenate([merged[i] for i in group], axis=1)
+        b = jnp.concatenate([start[i] for i in group], axis=1)
+        return lax.dot_general(a, b, (((1,), (1,)), ((), ())), preferred_element_type=F32)
+
     total = jnp.zeros((2 * ROWS, 128), F32)
-    for i in range(PARTS):
-        for copy in loads[i]:
-            copy.wait()
-        both = g_buf[i].astype(F32) + e_buf[i]
-        both_ref[i] = both
-        upper, lower = split(both, 2)
-        merged[i, 0:ROWS, :] = upper
-        merged[i, ROWS : 2 * ROWS, :] = lower
-        total = total + lax.dot_general(
-            merged[i], start[i], (((1,), (1,)), ((), ())), preferred_element_type=F32
-        )
+    for n, group in enumerate(GROUPS):
+        for i in group:
+            for copy in loads[i]:
+                copy.wait()
+        for i in group:
+            both = g_buf[i].astype(F32) + e_buf[i]
+            both_ref[i] = both
+            upper, lower = split(both, 2)
+            merged[i, 0:ROWS, :] = upper
+            merged[i, ROWS : 2 * ROWS, :] = lower
+        if n:
+            total = total + product(GROUPS[n - 1])
+    total = total + product(GROUPS[-1])
     left = total[0:ROWS] + total[ROWS : 2 * ROWS]
     turned = jnp.transpose(jnp.concatenate([left, jnp.zeros((64, 128), F32)], axis=0))
     left = (turned[0:RANK] + turned[RANK : 2 * RANK]) * 1.024
@@ -143,7 +155,7 @@
         for s in range(4):
             left_tiles[4 * t + s] = left[8 * s : 8 * s + 8, 128 * t : 128 * t + 128]
 
-    pl.semaphore_wait(barrier, DP + MP - 2 + (XS - 1) * (YS - 1))
+    pl.semaphore_wait(barrier, len(peers))
 
     def remote(src, dst, send, recv, device):
         return pltpu.make_async_remote_copy(
@@ -155,9 +167,8 @@
 
     left_owner = y == lax.rem(z, YS)
 
-    @pl.loop(0, ROW_TILES)
-    def _(k):
-        tile = lax.rem(z + k, ROW_TILES)
+    for dz in FAR_Z:
+        tile = lax.rem(z + dz, ROW_TILES)
         owner = tile * YS + lax.rem(tile, YS)
 
         @pl.when(owner != me)
@@ -170,9 +181,8 @@
         wait_bytes(left_in.at[pl.ds(0, DP - 1)], lt_recv)
         left_all[z] = jnp.sum(left_in[...], axis=0)
 
-        @pl.loop(1, DP)
-        def _(k):
-            remote(left_all.at[z], left_all.at[z], la_send, la_recv, (lax.rem(me + k, DP), mp)).start()
+        for d in FAR_DP:
+            remote(left_all.at[z], left_all.at[z], la_send, la_recv, over_dp(*d)).start()
 
         wait_bytes(left_all.at[pl.ds(0, ROW_TILES - 1)], la_recv)
 
@@ -199,42 +209,70 @@
 
     send_gram(gram_in, 0, left0)
 
-    pieces = jnp.concatenate(split(left0[:, 0:ROWS], 3), axis=0)
-
-    def right_part(into, part):
-        one = dot(pieces, merged[part, 0:ROWS, :])
-        two = dot(pieces[0 : 2 * RANK], merged[part, ROWS : 2 * ROWS, :])
-        value = (one[0:32] + (one[32:64] + two[0:32])) + (one[64:96] + two[32:64])
+    pieces = jnp.concatenate([p.astype(F32) for p in split(left0[:, 0:ROWS], 3)], axis=0)
+    pieces = jnp.concatenate([pieces, pieces], axis=1).astype(BF16)
+    mine = core * XS + x
+    streams = (
+        (core_out_a, core_in_a, own_a, xy_in_a, z_in_a, full_a),
+        (core_out_b, core_in_b, own_b, xy_in_b, z_in_b, full_b),
+    )
+
+    def right_part(into, part, columns):
+        value = dot(pieces, merged[part, :, columns])
+        value = value[0:32] + (value[32:64] + value[64:96])
         for s in range(YS):
             into[s] = value[8 * s : 8 * s + 8]
 
-    order = (2, 1, 3, 0)
-    for k in order:
-        right_part(core_out.at[k], (1 - core) * XS + lax.rem(x + k, XS))
-        remote(core_out.at[k], core_in.at[k], core_send, core_recv.at[k], sibling).start()
-    for k in order:
-        right_part(own.at[k], core * XS + lax.rem(x + k, XS))
-
-    for kx in order:
-        wait_bytes(core_in.at[kx], core_recv.at[kx])
-        own[kx] = own[kx] + core_in[kx]
-        for ky in (2, 1, 3, 0):
-            if kx or ky:
-                slot = kx * YS + ky - 1
-                remote(
-                    own.at[kx, lax.rem(y + ky, YS)], xy_in.at[slot], xy_send, xy_recv, plane(kx, ky)
-                ).start()
+    def products(n):
+        core_out, core_in, own = streams[n][0:3]
+        columns = slice(STREAMS[n][0], sum(STREAMS[n]))
+        for k in FAR:
+            right_part(core_out.at[k], (1 - core) * XS + lax.rem(x + k, XS), columns)
+            remote(core_out.at[k], core_in.at[k], core_send.at[n], core_recv.at[n, k], sibling).start()
+        for k in FAR:
+            right_part(own.at[k], core * XS + lax.rem(x + k, XS), columns)
+
+    def send_plane(n):
+        core_in, own, xy_in = streams[n][1:4]
+        for kx in FAR:
+            wait_bytes(core_in.at[kx], core_recv.at[n, kx])
+            own[kx] = own[kx] + core_in[kx]
+            for ky in FAR:
+                if kx or ky:
+                    remote(
+                        own.at[kx, lax.rem(y + ky, YS)], xy_in.at[kx * YS + ky - 1],
+                        xy_send.at[n], xy_recv.at[n], plane(kx, ky),
+                    ).start()
+
+    def send_z(n):
+        own, xy_in, z_in = streams[n][2:5]
+        wait_bytes(xy_in, xy_recv.at[n])
+        z_in[z] = own[0, y] + jnp.sum(xy_in[...], axis=0)
+        for dz in FAR_Z[:-1]:
+            remote(z_in.at[z], z_in.at[z], z_send.at[n], z_recv.at[n], over_dp(dz, 0)).start()
+
+    def gather_plane(n):
+        z_in, full = streams[n][4:6]
+        wait_bytes(z_in.at[pl.ds(0, ZS - 1)], z_recv.at[n])
+        full[mine, y] = jnp.sum(z_in[...], axis=0)
+        for kx in FAR:
+            for ky in FAR:
+                if kx or ky:
+                    remote(
+                        full.at[mine, y], full.at[mine, y], ag_send.at[n], ag_recv.at[n, kx], plane(kx, ky)
+                    ).start()
+
+    products(0)
+    send_plane(0)
+    products(1)
+    send_plane(1)
 
     inverse1 = inverse_cholesky(take_gram(gram_in, 0))
     left1 = full_dot(inverse1, left0)
     send_gram(gram_in2, 1, left1)
 
-    wait_bytes(xy_in, xy_recv)
-    z_in[z] = own[0, y] + jnp.sum(xy_in[...], axis=0)
-
-    @pl.loop(1, ROW_TILES)
-    def _(k):
-        remote(z_in.at[z], z_in.at[z], z_send, z_recv, (lax.rem(z + k, 8) * YS + y, mp)).start()
+    send_z(0)
+    send_z(1)
 
     inverse2 = inverse_cholesky(take_gram(gram_in2, 1))
     left2 = full_dot(inverse2, left1)[:, 0:ROWS]
@@ -244,26 +282,27 @@
     mix = jnp.transpose(jnp.pad(mix, ((0, 96), (0, 96))))[0:RANK]
     mix = jnp.transpose(stack_left(mix)).astype(BF16)[0:RANK]
 
-    mine = core * XS + x
-    wait_bytes(z_in.at[pl.ds(0, 7)], z_recv)
-    full[mine, y] = jnp.sum(z_in[...], axis=0)
-    for kx in order:
-        for ky in (2, 1, 3, 0):
-            if kx or ky:
-                remote(full.at[mine, y], full.at[mine, y], ag_send, ag_recv.at[kx], plane(kx, ky)).start()
-
-    def right_of(part):
-        sums = jnp.concatenate([full[part, s] for s in range(4)], axis=0)
-        right_ref[part] = dot(mix, stack_right(sums)) * (1.0 / DP)
-
-    for kx in (0, 1, 3, 2):
-        got = core * XS + lax.rem(x + XS - kx, XS)
-        wait_bytes(full.at[0, pl.ds(0, YS if kx else YS - 1)], ag_recv.at[kx])
-        remote(full.at[got], full.at[got], ac_send, ac_recv.at[kx], sibling).start()
-        right_of(got)
-    for kx in (0, 1, 3, 2):
-        wait_bytes(full.at[0], ac_recv.at[kx])
-        right_of((1 - core) * XS + lax.rem(x + XS - kx, XS))
+    gather_plane(0)
+    gather_plane(1)
+
+    def right_of(n, part):
+        columns = slice(STREAMS[n][0], sum(STREAMS[n]))
+        sums = jnp.concatenate([streams[n][5][part, s] for s in range(4)], axis=0)
+        right_ref[part, :, columns] = dot(mix, stack_right(sums)) * (1.0 / DP)
+
+    near = (0, 1, 3, 2)
+    for n in range(2):
+        full = streams[n][5]
+        for kx in near:
+            got = core * XS + lax.rem(x + XS - kx, XS)
+            wait_bytes(full.at[0, pl.ds(0, YS if kx else YS - 1)], ag_recv.at[n, kx])
+            remote(full.at[got], full.at[got], ac_send.at[n], ac_recv.at[n, kx], sibling).start()
+            right_of(n, got)
+    for n in range(2):
+        full = streams[n][5]
+        for kx in near:
+            wait_bytes(full.at[0], ac_recv.at[n, kx])
+            right_of(n, (1 - core) * XS + lax.rem(x + XS - kx, XS))
 
     @pl.when(left_owner)
     def _():
@@ -276,11 +315,12 @@
 
     for which in range(2):
         wait_bytes(left_in.at[pl.ds(0, MP - 1)], gr_send.at[which])
-    wait_bytes(core_out, core_send)
-    wait_bytes(xy_in, xy_send)
-    wait_bytes(z_in.at[pl.ds(0, 7)], z_send)
-    wait_bytes(xy_in, ag_send)
-    wait_bytes(core_out, ac_send)
+    for n, (core_out, _, _, xy_in, z_in, _) in enumerate(streams):
+        wait_bytes(core_out, core_send.at[n])
+        wait_bytes(xy_in, xy_send.at[n])
+        wait_bytes(z_in.at[pl.ds(0, ZS - 1)], z_send.at[n])
+        wait_bytes(xy_in, ag_send.at[n])
+        wait_bytes(core_out, ac_send.at[n])
 
 
 def run_exchange(gradients, errors, seeds):
@@ -308,17 +348,16 @@
             pltpu.VMEM((ROW_TILES, 8, 128), F32),
             pltpu.VMEM((MP, 8, 128), F32),
             pltpu.VMEM((MP, 8, 128), F32),
-            pltpu.VMEM((XS, YS, 8, WIDE), F32),
-            pltpu.VMEM((XS, YS, 8, WIDE), F32),
-            pltpu.VMEM((XS, YS, 8, WIDE), F32),
-            pltpu.VMEM((XS * YS - 1, 8, WIDE), F32),
-            pltpu.VMEM((DP // YS, 8, WIDE), F32),
-            pltpu.VMEM((PARTS, YS, 8, WIDE), F32),
+            *(
+                pltpu.VMEM(shape + (8, width), F32)
+                for _, width in STREAMS
+                for shape in ((XS, YS), (XS, YS), (XS, YS), (XS * YS - 1,), (ZS,), (PARTS, YS))
+            ),
             dma((2, PARTS)),
             dma,
             dma, dma, dma, dma, dma((2,)), dma((2,)),
-            dma, dma((XS,)), dma, dma, dma, dma,
-            dma, dma((XS,)), dma, dma((XS,)),
+            dma((2,)), dma((2, XS)), dma((2,)), dma((2,)), dma((2,)), dma((2,)),
+            dma((2,)), dma((2, XS)), dma((2,)), dma((2, XS)),
         ],
         compiler_params=pltpu.CompilerParams(
             collective_id=0, has_side_effects=True, vmem_limit_bytes=40 * 1024 * 1024

time: 53.4 us -> 49.9 us (0.934)
  Pallas kernels: 52.7 us -> 49.2 us
    pallas_call x1, Pallas kernels: 49.5 us -> 45.9 us  [run_exchange(): pl.pallas_call(exchange, out_shape=(jax.ShapeDtypeStruct((PARTS, ROWS, WI...]
where the time goes in v3:
time: 49.9 us; the launch traced here: 49.8 us
  Pallas kernels  49.2 us (99%)
  between operations  0.64 us (1%)
    pallas_call x1, Pallas kernels, run_exchange(): pl.pallas_call(exchange, out_shape=(jax.ShapeDtypeStruct((PARTS, ROWS, WI...  45.9 us
    pallas_call x1, Pallas kernels, run_finish(): pl.pallas_call(finish, out_shape=(jax.ShapeDtypeStruct((ROWS, COLS), F32)...  3.21 us

profile of v3, /device:TPU:1, one launch (start us, length us, event | category | flops | bytes accessed | tf_op | source)
XLA Modules:
  0.0 49.8 jit_solution(12568763007508947847)
XLA Ops:
  0.6 45.9 %exchange.1 = (f32[8,192,640]{2,1,0:T(8,128)S(1)}, f32[8,32,640]{2,1,0:T(8,128)S(1)}, bf16[192,192]{1,0:T(8,128)(2,1)S(1)}, f32[32,192]{1,0:T(8,128)S(1)}) custom-call(bf16[192,5120]{1,0:T(8,128)(2,1)} %bitcast.7, f32[192,5120]{1,0:T(8,128)} %bitcast.6, s32[32,5120]{1,0:T(8,128)} %bitcast.8), custom_call_target="tpu_custom_call" | custom-call | flops 1000000000 | bytes 8000000 | tf_op jit(solution)/shard_map/exchange/pallas_call | solution.py:330
  46.6 3.2 %finish.1 = (f32[192,5120]{1,0:T(8,128)}, bf16[192,5120]{1,0:T(8,128)(2,1)}, f32[32,5120]{1,0:T(8,128)}, f32[32,192]{1,0:T(8,128)}) custom-call(f32[8,192,640]{2,1,0:T(8,128)S(1)} %get-tuple-element.12.both_ref, f32[8,32,640]{2,1,0:T(8,128)S(1)} %get-tuple-element.13.right_ref, bf16[192,192]{1,0:T(8,128)(2,1)S(1)} %get-tuple-element.14.wide_ref, ...), custom_call_target="tpu_custom_call" | custom-call | flops 1000000000 | bytes 10000000 | tf_op jit(solution)/shard_map/finish/pallas_call | solution.py:396

commit v4 on v3

--- a/solution.py
+++ b/solution.py
@@ -13,16 +13,13 @@
 DP, MP, XS, YS = 32, 8, 4, 4
 PARTS = 8
 WIDE = COLS // PARTS
-ROW_TILES = 8
+ROW_TILES = 6
 STREAMS = ((0, 384), (384, 256))
 GROUPS = ((0, 1), (2, 3), (4, 5), (6,), (7,))
 ZS = DP // YS
 FAR_Z = (4, 3, 5, 2, 6, 1, 7, 0)
 FAR = (2, 1, 3, 0)
-FAR_DP = sorted(
-    ((dz, dy) for dz in range(ZS) for dy in range(YS) if dz or dy),
-    key=lambda d: -min(d[0], ZS - d[0]) - min(d[1], YS - d[1]),
-)
+LAG = 2
 
 
 def split(value, parts):
@@ -76,12 +73,12 @@
 def exchange(
     g_hbm, e_hbm, seed_hbm, both_ref, right_ref, wide_ref, left_ref,
     g_buf, e_buf, seed_buf, start, merged,
-    left_tiles, left_in, left_all,
+    left_y, left_z,
     gram_in, gram_in2,
     core_out_a, core_in_a, own_a, xy_in_a, z_in_a, full_a,
     core_out_b, core_in_b, own_b, xy_in_b, z_in_b, full_b,
     load_sem, seed_sem,
-    lt_send, lt_recv, la_send, la_recv, gr_send, gr_recv,
+    ly_send, ly_recv, lz_send, lz_recv, gr_send, gr_recv,
     core_send, core_recv, xy_send, xy_recv, z_send, z_recv,
     ag_send, ag_recv, ac_send, ac_recv,
 ):
@@ -100,8 +97,8 @@
     barrier = pltpu.get_barrier_semaphore()
     seed_copy = pltpu.make_async_copy(seed_hbm, seed_buf, seed_sem)
     seed_copy.start()
-    peers = [over_dp(*d) for d in FAR_DP] + [plane(kx, ky) for kx in FAR[:3] for ky in FAR[:3]]
-    peers += [(me, lax.rem(mp + k, MP)) for k in range(1, MP)]
+    peers = [over_dp(dz, 0) for dz in FAR_Z[:-1]] + [plane(kx, ky) for kx in FAR[:3] for ky in FAR[:3]]
+    peers += [over_dp(0, dy) for dy in FAR[:3]] + [(me, lax.rem(mp + k, MP)) for k in range(1, MP)]
     for peer in peers:
         pl.semaphore_signal(barrier, inc=1, device_id=peer, device_id_type=MESH)
 
@@ -124,17 +121,16 @@
     take = jnp.where(jnp.logical_and(shorter, jnp.logical_not(first)), 1.0, 0.0)
     seeds = seeds - take * seeds[0:1, :]
     high, low = split(seeds, 2)
-    blank = jnp.zeros((64, WIDE), BF16)
     for i in range(PARTS):
         columns = slice(i * WIDE, (i + 1) * WIDE)
-        start[i] = jnp.concatenate([high[:, columns], low[:, columns], blank], axis=0)
+        start[i] = jnp.concatenate([high[:, columns], low[:, columns]], axis=0)
 
     def product(group):
         a = jnp.concatenate([merged[i] for i in group], axis=1)
         b = jnp.concatenate([start[i] for i in group], axis=1)
         return lax.dot_general(a, b, (((1,), (1,)), ((), ())), preferred_element_type=F32)
 
-    total = jnp.zeros((2 * ROWS, 128), F32)
+    total = jnp.zeros((2 * ROWS, 64), F32)
     for n, group in enumerate(GROUPS):
         for i in group:
             for copy in loads[i]:
@@ -149,11 +145,13 @@
             total = total + product(GROUPS[n - 1])
     total = total + product(GROUPS[-1])
     left = total[0:ROWS] + total[ROWS : 2 * ROWS]
-    turned = jnp.transpose(jnp.concatenate([left, jnp.zeros((64, 128), F32)], axis=0))
+    turned = jnp.transpose(jnp.pad(left, ((0, 64), (0, 64))))
     left = (turned[0:RANK] + turned[RANK : 2 * RANK]) * 1.024
-    for t in range(2):
-        for s in range(4):
-            left_tiles[4 * t + s] = left[8 * s : 8 * s + 8, 128 * t : 128 * t + 128]
+    for s in range(4):
+        left_y[y, s] = left[8 * s : 8 * s + 8, 0:128]
+    for s in range(2):
+        rest = left[16 * s : 16 * s + 16, 128:256]
+        left_y[y, 4 + s] = rest[0:8] + pltpu.roll(rest[8:16], 64, 1)
 
     pl.semaphore_wait(barrier, len(peers))
 
@@ -165,33 +163,18 @@
     def wait_bytes(ref, sem):
         pltpu.make_async_copy(ref, ref, sem).wait()
 
-    left_owner = y == lax.rem(z, YS)
-
-    for dz in FAR_Z:
-        tile = lax.rem(z + dz, ROW_TILES)
-        owner = tile * YS + lax.rem(tile, YS)
-
-        @pl.when(owner != me)
-        def _():
-            remote(left_tiles.at[tile], left_in.at[me], lt_send, lt_recv, (owner, mp)).start()
-
-    @pl.when(left_owner)
-    def _():
-        left_in[me] = left_tiles[z]
-        wait_bytes(left_in.at[pl.ds(0, DP - 1)], lt_recv)
-        left_all[z] = jnp.sum(left_in[...], axis=0)
-
-        for d in FAR_DP:
-            remote(left_all.at[z], left_all.at[z], la_send, la_recv, over_dp(*d)).start()
-
-        wait_bytes(left_all.at[pl.ds(0, ROW_TILES - 1)], la_recv)
-
-    @pl.when(jnp.logical_not(left_owner))
-    def _():
-        wait_bytes(left_all.at[pl.ds(0, ROW_TILES)], la_recv)
-
+    for dy in FAR[:3]:
+        remote(left_y.at[y], left_y.at[y], ly_send, ly_recv, over_dp(0, dy)).start()
+    wait_bytes(left_y.at[pl.ds(0, YS - 1)], ly_recv)
+    left_z[z] = jnp.sum(left_y[...], axis=0)
+    for dz in FAR_Z[:-1]:
+        remote(left_z.at[z], left_z.at[z], lz_send, lz_recv, over_dp(dz, 0)).start()
+    wait_bytes(left_z.at[pl.ds(0, ZS - 1)], lz_recv)
+    left = jnp.sum(left_z[...], axis=0)
+    half = lax.broadcasted_iota(jnp.int32, (8, 128), 1) < 64
+    rest = [jnp.where(half, v, 0.0) for t in (4, 5) for v in (left[t], pltpu.roll(left[t], 64, 1))]
     left0 = jnp.concatenate(
-        [jnp.concatenate([left_all[4 * t + s] for s in range(4)], axis=0) for t in range(2)], axis=1
+        [jnp.concatenate([left[s] for s in range(4)], axis=0), jnp.concatenate(rest, axis=0)], axis=1
     )
 
     def send_gram(slots, which, value):
@@ -223,26 +206,23 @@
         for s in range(YS):
             into[s] = value[8 * s : 8 * s + 8]
 
-    def products(n):
+    def products(n, k):
         core_out, core_in, own = streams[n][0:3]
         columns = slice(STREAMS[n][0], sum(STREAMS[n]))
-        for k in FAR:
-            right_part(core_out.at[k], (1 - core) * XS + lax.rem(x + k, XS), columns)
-            remote(core_out.at[k], core_in.at[k], core_send.at[n], core_recv.at[n, k], sibling).start()
-        for k in FAR:
-            right_part(own.at[k], core * XS + lax.rem(x + k, XS), columns)
-
-    def send_plane(n):
+        right_part(core_out.at[k], (1 - core) * XS + lax.rem(x + k, XS), columns)
+        remote(core_out.at[k], core_in.at[k], core_send.at[n], core_recv.at[n, k], sibling).start()
+        right_part(own.at[k], core * XS + lax.rem(x + k, XS), columns)
+
+    def send_plane(n, kx):
         core_in, own, xy_in = streams[n][1:4]
-        for kx in FAR:
-            wait_bytes(core_in.at[kx], core_recv.at[n, kx])
-            own[kx] = own[kx] + core_in[kx]
-            for ky in FAR:
-                if kx or ky:
-                    remote(
-                        own.at[kx, lax.rem(y + ky, YS)], xy_in.at[kx * YS + ky - 1],
-                        xy_send.at[n], xy_recv.at[n], plane(kx, ky),
-                    ).start()
+        wait_bytes(core_in.at[kx], core_recv.at[n, kx])
+        own[kx] = own[kx] + core_in[kx]
+        for ky in FAR:
+            if kx or ky:
+                remote(
+                    own.at[kx, lax.rem(y + ky, YS)], xy_in.at[kx * YS + ky - 1],
+                    xy_send.at[n], xy_recv.at[n], plane(kx, ky),
+                ).start()
 
     def send_z(n):
         own, xy_in, z_in = streams[n][2:5]
@@ -262,17 +242,23 @@
                         full.at[mine, y], full.at[mine, y], ag_send.at[n], ag_recv.at[n, kx], plane(kx, ky)
                     ).start()
 
-    products(0)
-    send_plane(0)
-    products(1)
-    send_plane(1)
+    chunks = [(n, k) for n in range(2) for k in FAR]
+    for i, chunk in enumerate(chunks):
+        products(*chunk)
+        if i >= LAG:
+            send_plane(*chunks[i - LAG])
+    for chunk in chunks[-LAG:]:
+        send_plane(*chunk)
+
+    send_z(0)
+    send_z(1)
 
     inverse1 = inverse_cholesky(take_gram(gram_in, 0))
     left1 = full_dot(inverse1, left0)
     send_gram(gram_in2, 1, left1)
 
-    send_z(0)
-    send_z(1)
+    gather_plane(0)
+    gather_plane(1)
 
     inverse2 = inverse_cholesky(take_gram(gram_in2, 1))
     left2 = full_dot(inverse2, left1)[:, 0:ROWS]
@@ -281,9 +267,6 @@
     mix = full_dot(inverse2, inverse1)
     mix = jnp.transpose(jnp.pad(mix, ((0, 96), (0, 96))))[0:RANK]
     mix = jnp.transpose(stack_left(mix)).astype(BF16)[0:RANK]
-
-    gather_plane(0)
-    gather_plane(1)
 
     def right_of(n, part):
         columns = slice(STREAMS[n][0], sum(STREAMS[n]))
@@ -304,17 +287,10 @@
             wait_bytes(full.at[0], ac_recv.at[n, kx])
             right_of(n, (1 - core) * XS + lax.rem(x + XS - kx, XS))
 
-    @pl.when(left_owner)
-    def _():
-        wait_bytes(left_in.at[pl.ds(0, ROW_TILES - 1)], lt_send)
-        wait_bytes(left_in.at[pl.ds(0, DP - 1)], la_send)
-
-    @pl.when(jnp.logical_not(left_owner))
-    def _():
-        wait_bytes(left_in.at[pl.ds(0, ROW_TILES)], lt_send)
-
+    wait_bytes(left_y.at[pl.ds(0, YS - 1)], ly_send)
+    wait_bytes(left_z.at[pl.ds(0, ZS - 1)], lz_send)
     for which in range(2):
-        wait_bytes(left_in.at[pl.ds(0, MP - 1)], gr_send.at[which])
+        wait_bytes(gram_in.at[pl.ds(0, MP - 1)], gr_send.at[which])
     for n, (core_out, _, _, xy_in, z_in, _) in enumerate(streams):
         wait_bytes(core_out, core_send.at[n])
         wait_bytes(xy_in, xy_send.at[n])
@@ -341,11 +317,10 @@
             pltpu.VMEM((PARTS, ROWS, WIDE), BF16),
             pltpu.VMEM((PARTS, ROWS, WIDE), F32),
             pltpu.VMEM((RANK, COLS), jnp.int32),
-            pltpu.VMEM((PARTS, 128, WIDE), BF16),
+            pltpu.VMEM((PARTS, 64, WIDE), BF16),
             pltpu.VMEM((PARTS, 2 * ROWS, WIDE), BF16),
-            pltpu.VMEM((ROW_TILES, 8, 128), F32),
-            pltpu.VMEM((DP, 8, 128), F32),
-            pltpu.VMEM((ROW_TILES, 8, 128), F32),
+            pltpu.VMEM((YS, ROW_TILES, 8, 128), F32),
+            pltpu.VMEM((ZS, ROW_TILES, 8, 128), F32),
             pltpu.VMEM((MP, 8, 128), F32),
             pltpu.VMEM((MP, 8, 128), F32),
             *(

time: 49.9 us -> 47.7 us (0.956)
  Pallas kernels: 49.2 us -> 47 us
    pallas_call x1, Pallas kernels: 45.9 us -> 43.7 us  [run_exchange(): pl.pallas_call(exchange, out_shape=(jax.ShapeDtypeStruct((PARTS, ROWS, WI...]
where the time goes in v4:
time: 47.7 us; the launch traced here: 47.6 us
  Pallas kernels  47 us (99%)
  between operations  0.64 us (1%)
    pallas_call x1, Pallas kernels, run_exchange(): pl.pallas_call(exchange, out_shape=(jax.ShapeDtypeStruct((PARTS, ROWS, WI...  43.7 us
    pallas_call x1, Pallas kernels, run_finish(): pl.pallas_call(finish, out_shape=(jax.ShapeDtypeStruct((ROWS, COLS), F32)...  3.21 us

profile of v4, /device:TPU:1, one launch (start us, length us, event | category | flops | bytes accessed | tf_op | source)
XLA Modules:
  0.0 47.6 jit_solution(12968844696029430616)
XLA Ops:
  0.6 43.7 %exchange.1 = (f32[8,192,640]{2,1,0:T(8,128)S(1)}, f32[8,32,640]{2,1,0:T(8,128)S(1)}, bf16[192,192]{1,0:T(8,128)(2,1)S(1)}, f32[32,192]{1,0:T(8,128)S(1)}) custom-call(bf16[192,5120]{1,0:T(8,128)(2,1)} %bitcast.7, f32[192,5120]{1,0:T(8,128)} %bitcast.6, s32[32,5120]{1,0:T(8,128)} %bitcast.8), custom_call_target="tpu_custom_call" | custom-call | flops 1000000000 | bytes 8000000 | tf_op jit(solution)/shard_map/exchange/pallas_call | solution.py:306
  44.4 3.2 %finish.1 = (f32[192,5120]{1,0:T(8,128)}, bf16[192,5120]{1,0:T(8,128)(2,1)}, f32[32,5120]{1,0:T(8,128)}, f32[32,192]{1,0:T(8,128)}) custom-call(f32[8,192,640]{2,1,0:T(8,128)S(1)} %get-tuple-element.12.both_ref, f32[8,32,640]{2,1,0:T(8,128)S(1)} %get-tuple-element.13.right_ref, bf16[192,192]{1,0:T(8,128)(2,1)S(1)} %get-tuple-element.14.wide_ref, ...), custom_call_target="tpu_custom_call" | custom-call | flops 1000000000 | bytes 10000000 | tf_op jit(solution)/shard_map/finish/pallas_call | solution.py:371

commit v5 on v4

--- a/solution.py
+++ b/solution.py
@@ -19,7 +19,6 @@
 ZS = DP // YS
 FAR_Z = (4, 3, 5, 2, 6, 1, 7, 0)
 FAR = (2, 1, 3, 0)
-LAG = 2
 
 
 def split(value, parts):
@@ -44,10 +43,15 @@
     lane_id = lax.broadcasted_iota(jnp.int32, (RANK, 128), 1)
     table = jnp.concatenate([gram, jnp.zeros((RANK, 128 - RANK), F32)], axis=1)
     table = table + jnp.where(lane_id == row_id + RANK, 1.0, 0.0)
+    blocks = [table[8 * i : 8 * i + 8] for i in range(4)]
     for j in range(RANK - 1):
-        row = table[j : j + 1, :] / table[j : j + 1, j : j + 1]
-        column = jnp.where(row_id > j, table[:, j : j + 1], 0.0)
-        table = table - column * row
+        at, within = j // 8, j % 8
+        columns = {i: jnp.broadcast_to(blocks[i][:, j : j + 1], (8, 128)) for i in range(at, 4)}
+        row = blocks[at][within : within + 1] * (1.0 / columns[at][within : within + 1])
+        columns[at] = jnp.where(row_id[0:8] > within, columns[at], 0.0)
+        for i, column in columns.items():
+            blocks[i] = blocks[i] - column * row
+    table = jnp.concatenate(blocks, axis=0)
     pivots = jnp.sum(jnp.where(lane_id == row_id, table, 0.0), axis=1, keepdims=True)
     return table[:, RANK : 2 * RANK] / jnp.sqrt(pivots)
 
@@ -73,13 +77,13 @@
 def exchange(
     g_hbm, e_hbm, seed_hbm, both_ref, right_ref, wide_ref, left_ref,
     g_buf, e_buf, seed_buf, start, merged,
-    left_y, left_z,
+    left_y, left_z, left_mine, left_other, other, other_split,
     gram_in, gram_in2,
-    core_out_a, core_in_a, own_a, xy_in_a, z_in_a, full_a,
-    core_out_b, core_in_b, own_b, xy_in_b, z_in_b, full_b,
+    own_a, xy_in_a, z_in_a, full_a,
+    own_b, xy_in_b, z_in_b, full_b,
     load_sem, seed_sem,
     ly_send, ly_recv, lz_send, lz_recv, gr_send, gr_recv,
-    core_send, core_recv, xy_send, xy_recv, z_send, z_recv,
+    lc_send, lc_recv, oc_send, oc_recv, xy_send, xy_recv, z_send, z_recv,
     ag_send, ag_recv, ac_send, ac_recv,
 ):
     me = lax.axis_index("dp")
@@ -165,17 +169,30 @@
 
     for dy in FAR[:3]:
         remote(left_y.at[y], left_y.at[y], ly_send, ly_recv, over_dp(0, dy)).start()
+    for k in FAR:
+        part = (1 - core) * XS + lax.rem(x + k, XS)
+        remote(both_ref.at[part], other.at[k], oc_send, oc_recv, sibling).start()
     wait_bytes(left_y.at[pl.ds(0, YS - 1)], ly_recv)
     left_z[z] = jnp.sum(left_y[...], axis=0)
     for dz in FAR_Z[:-1]:
         remote(left_z.at[z], left_z.at[z], lz_send, lz_recv, over_dp(dz, 0)).start()
+    wait_bytes(other, oc_recv)
+    for k in range(XS):
+        upper, lower = split(other[k], 2)
+        other_split[k, 0:ROWS, :] = upper
+        other_split[k, ROWS : 2 * ROWS, :] = lower
     wait_bytes(left_z.at[pl.ds(0, ZS - 1)], lz_recv)
-    left = jnp.sum(left_z[...], axis=0)
+    left_mine[...] = jnp.sum(left_z[...], axis=0)
+    remote(left_mine, left_other, lc_send, lc_recv, sibling).start()
     half = lax.broadcasted_iota(jnp.int32, (8, 128), 1) < 64
-    rest = [jnp.where(half, v, 0.0) for t in (4, 5) for v in (left[t], pltpu.roll(left[t], 64, 1))]
-    left0 = jnp.concatenate(
-        [jnp.concatenate([left[s] for s in range(4)], axis=0), jnp.concatenate(rest, axis=0)], axis=1
-    )
+
+    def matrix(tiles):
+        rest = [jnp.where(half, v, 0.0) for t in (4, 5) for v in (tiles[t], pltpu.roll(tiles[t], 64, 1))]
+        return jnp.concatenate(
+            [jnp.concatenate([tiles[s] for s in range(4)], axis=0), jnp.concatenate(rest, axis=0)], axis=1
+        )
+
+    left0 = matrix(left_mine)
 
     def send_gram(slots, which, value):
         slots[mp] = pack(full_dot(value, value, ((1,), (1,))))
@@ -192,31 +209,31 @@
 
     send_gram(gram_in, 0, left0)
 
-    pieces = jnp.concatenate([p.astype(F32) for p in split(left0[:, 0:ROWS], 3)], axis=0)
-    pieces = jnp.concatenate([pieces, pieces], axis=1).astype(BF16)
+    def pieces_of(left):
+        rows = jnp.concatenate([p.astype(F32) for p in split(left[:, 0:ROWS], 3)], axis=0)
+        return jnp.concatenate([rows, rows], axis=1).astype(BF16)
+
+    pieces = pieces_of(left0)
     mine = core * XS + x
     streams = (
-        (core_out_a, core_in_a, own_a, xy_in_a, z_in_a, full_a),
-        (core_out_b, core_in_b, own_b, xy_in_b, z_in_b, full_b),
+        (own_a, xy_in_a, z_in_a, full_a),
+        (own_b, xy_in_b, z_in_b, full_b),
     )
 
-    def right_part(into, part, columns):
-        value = dot(pieces, merged[part, :, columns])
-        value = value[0:32] + (value[32:64] + value[64:96])
+    def right_part(rows, values, n):
+        value = dot(rows, values[:, STREAMS[n][0] : sum(STREAMS[n])])
+        return value[0:32] + (value[32:64] + value[64:96])
+
+    def put(into, value, more):
         for s in range(YS):
-            into[s] = value[8 * s : 8 * s + 8]
-
-    def products(n, k):
-        core_out, core_in, own = streams[n][0:3]
-        columns = slice(STREAMS[n][0], sum(STREAMS[n]))
-        right_part(core_out.at[k], (1 - core) * XS + lax.rem(x + k, XS), columns)
-        remote(core_out.at[k], core_in.at[k], core_send.at[n], core_recv.at[n, k], sibling).start()
-        right_part(own.at[k], core * XS + lax.rem(x + k, XS), columns)
+            piece = value[8 * s : 8 * s + 8]
+            into[s] = into[s] + piece if more else piece
+
+    def my_rows(n, k):
+        return right_part(pieces, merged.at[core * XS + lax.rem(x + k, XS)], n)
 
     def send_plane(n, kx):
-        core_in, own, xy_in = streams[n][1:4]
-        wait_bytes(core_in.at[kx], core_recv.at[n, kx])
-        own[kx] = own[kx] + core_in[kx]
+        own, xy_in = streams[n][0:2]
         for ky in FAR:
             if kx or ky:
                 remote(
@@ -225,14 +242,14 @@
                 ).start()
 
     def send_z(n):
-        own, xy_in, z_in = streams[n][2:5]
+        own, xy_in, z_in = streams[n][0:3]
         wait_bytes(xy_in, xy_recv.at[n])
         z_in[z] = own[0, y] + jnp.sum(xy_in[...], axis=0)
         for dz in FAR_Z[:-1]:
             remote(z_in.at[z], z_in.at[z], z_send.at[n], z_recv.at[n], over_dp(dz, 0)).start()
 
     def gather_plane(n):
-        z_in, full = streams[n][4:6]
+        z_in, full = streams[n][2:4]
         wait_bytes(z_in.at[pl.ds(0, ZS - 1)], z_recv.at[n])
         full[mine, y] = jnp.sum(z_in[...], axis=0)
         for kx in FAR:
@@ -242,20 +259,24 @@
                         full.at[mine, y], full.at[mine, y], ag_send.at[n], ag_recv.at[n, kx], plane(kx, ky)
                     ).start()
 
-    chunks = [(n, k) for n in range(2) for k in FAR]
-    for i, chunk in enumerate(chunks):
-        products(*chunk)
-        if i >= LAG:
-            send_plane(*chunks[i - LAG])
-    for chunk in chunks[-LAG:]:
-        send_plane(*chunk)
-
-    send_z(0)
-    send_z(1)
+    for k in FAR:
+        put(own_a.at[k], my_rows(0, k), False)
+    wait_bytes(left_other, lc_recv)
+    pieces_other = pieces_of(matrix(left_other))
+    for n in range(2):
+        for k in FAR:
+            value = right_part(pieces_other, other_split.at[k], n)
+            if n:
+                value = value + my_rows(n, k)
+            put(streams[n][0].at[k], value, n == 0)
+            send_plane(n, k)
 
     inverse1 = inverse_cholesky(take_gram(gram_in, 0))
     left1 = full_dot(inverse1, left0)
     send_gram(gram_in2, 1, left1)
+
+    send_z(0)
+    send_z(1)
 
     gather_plane(0)
     gather_plane(1)
@@ -270,19 +291,21 @@
 
     def right_of(n, part):
         columns = slice(STREAMS[n][0], sum(STREAMS[n]))
-        sums = jnp.concatenate([streams[n][5][part, s] for s in range(4)], axis=0)
+        sums = jnp.concatenate([streams[n][3][part, s] for s in range(4)], axis=0)
         right_ref[part, :, columns] = dot(mix, stack_right(sums)) * (1.0 / DP)
 
     near = (0, 1, 3, 2)
     for n in range(2):
-        full = streams[n][5]
+        full = streams[n][3]
         for kx in near:
             got = core * XS + lax.rem(x + XS - kx, XS)
             wait_bytes(full.at[0, pl.ds(0, YS if kx else YS - 1)], ag_recv.at[n, kx])
             remote(full.at[got], full.at[got], ac_send.at[n], ac_recv.at[n, kx], sibling).start()
-            right_of(n, got)
     for n in range(2):
-        full = streams[n][5]
+        for kx in near:
+            right_of(n, core * XS + lax.rem(x + XS - kx, XS))
+    for n in range(2):
+        full = streams[n][3]
         for kx in near:
             wait_bytes(full.at[0], ac_recv.at[n, kx])
             right_of(n, (1 - core) * XS + lax.rem(x + XS - kx, XS))
@@ -291,12 +314,13 @@
     wait_bytes(left_z.at[pl.ds(0, ZS - 1)], lz_send)
     for which in range(2):
         wait_bytes(gram_in.at[pl.ds(0, MP - 1)], gr_send.at[which])
-    for n, (core_out, _, _, xy_in, z_in, _) in enumerate(streams):
-        wait_bytes(core_out, core_send.at[n])
+    wait_bytes(left_other, lc_send)
+    wait_bytes(other, oc_send)
+    for n, (_, xy_in, z_in, full) in enumerate(streams):
         wait_bytes(xy_in, xy_send.at[n])
         wait_bytes(z_in.at[pl.ds(0, ZS - 1)], z_send.at[n])
         wait_bytes(xy_in, ag_send.at[n])
-        wait_bytes(core_out, ac_send.at[n])
+        wait_bytes(full.at[pl.ds(0, XS)], ac_send.at[n])
 
 
 def run_exchange(gradients, errors, seeds):
@@ -321,17 +345,21 @@
             pltpu.VMEM((PARTS, 2 * ROWS, WIDE), BF16),
             pltpu.VMEM((YS, ROW_TILES, 8, 128), F32),
             pltpu.VMEM((ZS, ROW_TILES, 8, 128), F32),
+            pltpu.VMEM((ROW_TILES, 8, 128), F32),
+            pltpu.VMEM((ROW_TILES, 8, 128), F32),
+            pltpu.VMEM((XS, ROWS, WIDE), F32),
+            pltpu.VMEM((XS, 2 * ROWS, WIDE), BF16),
             pltpu.VMEM((MP, 8, 128), F32),
             pltpu.VMEM((MP, 8, 128), F32),
             *(
                 pltpu.VMEM(shape + (8, width), F32)
                 for _, width in STREAMS
-                for shape in ((XS, YS), (XS, YS), (XS, YS), (XS * YS - 1,), (ZS,), (PARTS, YS))
+                for shape in ((XS, YS), (XS * YS - 1,), (ZS,), (PARTS, YS))
             ),
             dma((2, PARTS)),
             dma,
             dma, dma, dma, dma, dma((2,)), dma((2,)),
-            dma((2,)), dma((2, XS)), dma((2,)), dma((2,)), dma((2,)), dma((2,)),
+            dma, dma, dma, dma, dma((2,)), dma((2,)), dma((2,)), dma((2,)),
             dma((2,)), dma((2, XS)), dma((2,)), dma((2, XS)),
         ],
         compiler_params=pltpu.CompilerParams(

time: 47.7 us -> 46.6 us (0.977)
  Pallas kernels: 47 us -> 45.9 us
    pallas_call x1, Pallas kernels: 43.7 us -> 42.7 us  [run_exchange(): pl.pallas_call(exchange, out_shape=(jax.ShapeDtypeStruct((PARTS, ROWS, WI...]
where the time goes in v5:
time: 46.6 us
  Pallas kernels  45.9 us (98%)
  between operations  0.64 us (1%)
    pallas_call x1, Pallas kernels, run_exchange(): pl.pallas_call(exchange, out_shape=(jax.ShapeDtypeStruct((PARTS, ROWS, WI...  42.7 us
    pallas_call x1, Pallas kernels, run_finish(): pl.pallas_call(finish, out_shape=(jax.ShapeDtypeStruct((ROWS, COLS), F32)...  3.21 us

profile of v5, /device:TPU:1, one launch (start us, length us, event | category | flops | bytes accessed | tf_op | source)
XLA Modules:
  0.0 46.6 jit_solution(3250897934000336486)
XLA Ops:
  0.6 42.7 %exchange.1 = (f32[8,192,640]{2,1,0:T(8,128)S(1)}, f32[8,32,640]{2,1,0:T(8,128)S(1)}, bf16[192,192]{1,0:T(8,128)(2,1)S(1)}, f32[32,192]{1,0:T(8,128)S(1)}) custom-call(bf16[192,5120]{1,0:T(8,128)(2,1)} %bitcast.7, f32[192,5120]{1,0:T(8,128)} %bitcast.6, s32[32,5120]{1,0:T(8,128)} %bitcast.8), custom_call_target="tpu_custom_call" | custom-call | flops 1000000000 | bytes 8000000 | tf_op jit(solution)/shard_map/exchange/pallas_call | solution.py:330
  43.4 3.2 %finish.1 = (f32[192,5120]{1,0:T(8,128)}, bf16[192,5120]{1,0:T(8,128)(2,1)}, f32[32,5120]{1,0:T(8,128)}, f32[32,192]{1,0:T(8,128)}) custom-call(f32[8,192,640]{2,1,0:T(8,128)S(1)} %get-tuple-element.12.both_ref, f32[8,32,640]{2,1,0:T(8,128)S(1)} %get-tuple-element.13.right_ref, bf16[192,192]{1,0:T(8,128)(2,1)S(1)} %get-tuple-element.14.wide_ref, ...), custom_call_target="tpu_custom_call" | custom-call | flops 1000000000 | bytes 10000000 | tf_op jit(solution)/shard_map/finish/pallas_call | solution.py:399

commit v6 on v5

--- a/solution.py
+++ b/solution.py
@@ -14,7 +14,7 @@
 PARTS = 8
 WIDE = COLS // PARTS
 ROW_TILES = 6
-STREAMS = ((0, 384), (384, 256))
+STREAMS = ((0, 256), (256, 384))
 GROUPS = ((0, 1), (2, 3), (4, 5), (6,), (7,))
 ZS = DP // YS
 FAR_Z = (4, 3, 5, 2, 6, 1, 7, 0)

time: 46.6 us -> 46.3 us (level)
  no operation moved by 1% of the time
where the time goes in v6:
time: 46.3 us; the launch traced here: 46.2 us
  Pallas kernels  45.5 us (98%)
  between operations  0.64 us (1%)
    pallas_call x1, Pallas kernels, run_exchange(): pl.pallas_call(exchange, out_shape=(jax.ShapeDtypeStruct((PARTS, ROWS, WI...  42.3 us
    pallas_call x1, Pallas kernels, run_finish(): pl.pallas_call(finish, out_shape=(jax.ShapeDtypeStruct((ROWS, COLS), F32)...  3.21 us

profile of v6, /device:TPU:1, one launch (start us, length us, event | category | flops | bytes accessed | tf_op | source)
XLA Modules:
  0.0 46.2 jit_solution(8349201423700457334)
XLA Ops:
  0.6 42.3 %exchange.1 = (f32[8,192,640]{2,1,0:T(8,128)S(1)}, f32[8,32,640]{2,1,0:T(8,128)S(1)}, bf16[192,192]{1,0:T(8,128)(2,1)S(1)}, f32[32,192]{1,0:T(8,128)S(1)}) custom-call(bf16[192,5120]{1,0:T(8,128)(2,1)} %bitcast.7, f32[192,5120]{1,0:T(8,128)} %bitcast.6, s32[32,5120]{1,0:T(8,128)} %bitcast.8), custom_call_target="tpu_custom_call" | custom-call | flops 1000000000 | bytes 8000000 | tf_op jit(solution)/shard_map/exchange/pallas_call | solution.py:330
  43.0 3.2 %finish.1 = (f32[192,5120]{1,0:T(8,128)}, bf16[192,5120]{1,0:T(8,128)(2,1)}, f32[32,5120]{1,0:T(8,128)}, f32[32,192]{1,0:T(8,128)}) custom-call(f32[8,192,640]{2,1,0:T(8,128)S(1)} %get-tuple-element.12.both_ref, f32[8,32,640]{2,1,0:T(8,128)S(1)} %get-tuple-element.13.right_ref, bf16[192,192]{1,0:T(8,128)(2,1)S(1)} %get-tuple-element.14.wide_ref, ...), custom_call_target="tpu_custom_call" | custom-call | flops 1000000000 | bytes 10000000 | tf_op jit(solution)/shard_map/finish/pallas_call | solution.py:399

commit v7 on v6

--- a/solution.py
+++ b/solution.py
@@ -14,7 +14,7 @@
 PARTS = 8
 WIDE = COLS // PARTS
 ROW_TILES = 6
-STREAMS = ((0, 256), (256, 384))
+STREAMS = ((0, 128), (128, 512))
 GROUPS = ((0, 1), (2, 3), (4, 5), (6,), (7,))
 ZS = DP // YS
 FAR_Z = (4, 3, 5, 2, 6, 1, 7, 0)

time: 46.3 us -> 47.4 us (1.024)
  Pallas kernels: 45.5 us -> 46.6 us
    pallas_call x1, Pallas kernels: 42.3 us -> 43.4 us  [run_exchange(): pl.pallas_call(exchange, out_shape=(jax.ShapeDtypeStruct((PARTS, ROWS, WI...]
where the time goes in v7:
time: 47.4 us; the launch traced here: 47.3 us
  Pallas kernels  46.6 us (98%)
  between operations  0.64 us (1%)
    pallas_call x1, Pallas kernels, run_exchange(): pl.pallas_call(exchange, out_shape=(jax.ShapeDtypeStruct((PARTS, ROWS, WI...  43.4 us
    pallas_call x1, Pallas kernels, run_finish(): pl.pallas_call(finish, out_shape=(jax.ShapeDtypeStruct((ROWS, COLS), F32)...  3.21 us

profile of v7, /device:TPU:1, one launch (start us, length us, event | category | flops | bytes accessed | tf_op | source)
XLA Modules:
  0.0 47.3 jit_solution(1060074845052817198)
XLA Ops:
  0.6 43.4 %exchange.1 = (f32[8,192,640]{2,1,0:T(8,128)S(1)}, f32[8,32,640]{2,1,0:T(8,128)S(1)}, bf16[192,192]{1,0:T(8,128)(2,1)S(1)}, f32[32,192]{1,0:T(8,128)S(1)}) custom-call(bf16[192,5120]{1,0:T(8,128)(2,1)} %bitcast.7, f32[192,5120]{1,0:T(8,128)} %bitcast.6, s32[32,5120]{1,0:T(8,128)} %bitcast.8), custom_call_target="tpu_custom_call" | custom-call | flops 1000000000 | bytes 8000000 | tf_op jit(solution)/shard_map/exchange/pallas_call | solution.py:330
  44.1 3.2 %finish.1 = (f32[192,5120]{1,0:T(8,128)}, bf16[192,5120]{1,0:T(8,128)(2,1)}, f32[32,5120]{1,0:T(8,128)}, f32[32,192]{1,0:T(8,128)}) custom-call(f32[8,192,640]{2,1,0:T(8,128)S(1)} %get-tuple-element.12.both_ref, f32[8,32,640]{2,1,0:T(8,128)S(1)} %get-tuple-element.13.right_ref, bf16[192,192]{1,0:T(8,128)(2,1)S(1)} %get-tuple-element.14.wide_ref, ...), custom_call_target="tpu_custom_call" | custom-call | flops 1000000000 | bytes 10000000 | tf_op jit(solution)/shard_map/finish/pallas_call | solution.py:399
